TPU v7x, 512 devices: a whole 4x4x16 slice. The times are simulated.
512 devices in a mesh: seq: 64 (over z, x_hi, core), head: 8 (over x_lo, y).
Axes of the slice: x: 4 (x_hi: 2, x_lo: 2; x = x_hi * 2 + x_lo), y: 4, z: 16, core: 2. Of those that a mesh axis runs over, the one named last changes fastest.
Arguments:
- events: bfloat16 [16384, 1024], P('seq'), may hold values from -60 to 60
- out_grad: bfloat16 [16384, 1024], P('seq', 'head'), may hold values from -16 to 16
- saved_attn: bfloat16 [16384, 1024], P('seq', 'head'), may hold values from -0.119628906 to 0.119628906
- in_weight: bfloat16 [1024, 4096], P(None, 'head'), may hold values from -0.1875 to 0.1875
- out_weight: bfloat16 [1024, 1024], P(None, 'head'), may hold values from -0.1875 to 0.1875
- lengths: int32 [16], replicated, may hold values from 1 to 4096, 16384 in all
Outputs:
- grad_in: bfloat16 [16384, 1024], P('seq', 'head')
- grad_w1: float32 [1024, 4096], P('seq', 'head')
- grad_w2: float32 [1024, 1024], P('seq', 'head')
Inputs may be any that keep to these rules, and one draw needn't show every extreme that they name: The 16 lengths sum to 16384 and the longest is exactly 4096.
All inputs are finite; a program needn't handle non-finite values.
Results may differ from a plain program's by a relative error of at most 0.0077.
Values may be sent and summed in bfloat16 or wider, within the bound.
A program may use at most 64 MiB of HBM per device.

v0:
```python
import math

import jax
import jax.numpy as jnp
from jax import lax
from jax.sharding import PartitionSpec as P

HEAD_DIM = 128


EPS = 1e-05


def shifted(x, axis, by):
    devices = lax.axis_size(axis)
    return lax.ppermute(x, axis, [(i, (i + by) % devices) for i in range(devices)])


def silu_slope(value):
    sig = jax.nn.sigmoid(value)
    return sig * (1.0 + value * (1.0 - sig))


def segment_of(position, lengths):
    ends = jnp.cumsum(lengths)
    return jnp.sum((position[:, None] >= ends[None, :]).astype(jnp.int32), axis=1)


def pair_terms(query_pair, query_pos, key_pair, key_pos, lengths, scale, norm):
    queries = query_pair[0]
    upstream = query_pair[1]
    keys = key_pair[0]
    values = key_pair[1]
    mask = (segment_of(query_pos, lengths)[:, None] == segment_of(key_pos, lengths)[None, :]) & (
        key_pos[None, :] <= query_pos[:, None]
    )
    empty_q = jnp.zeros(queries.shape, jnp.float32)
    empty_kv = jnp.zeros((2,) + keys.shape, jnp.float32)

    def work(unused):
        scores = (
            jnp.einsum("qhd,khd->hqk", queries, keys, preferred_element_type=jnp.float32) * scale
        )
        sig = jax.nn.sigmoid(scores)
        dprob = jnp.einsum("qhd,khd->hqk", upstream, values, preferred_element_type=jnp.float32)
        dscore = jnp.where(
            mask[None], dprob * sig * (1.0 + scores * (1.0 - sig)) / norm, 0.0
        ).astype(jnp.bfloat16)
        grad_q = (
            jnp.einsum("hqk,khd->qhd", dscore, keys, preferred_element_type=jnp.float32) * scale
        )
        weights = jnp.where(mask[None], scores * sig / norm, 0.0).astype(jnp.bfloat16)
        grad_k = (
            jnp.einsum("hqk,qhd->khd", dscore, queries, preferred_element_type=jnp.float32) * scale
        )
        grad_v = jnp.einsum("hqk,qhd->khd", weights, upstream, preferred_element_type=jnp.float32)
        grad_kv = jnp.stack((grad_k, grad_v))
        return (grad_q, grad_kv)

    def skip(unused):
        return (empty_q, empty_kv)

    return lax.cond(jnp.any(mask), work, skip, 0)


def per_device(events, out_grad, saved_attn, in_weight, out_weight, lengths):
    tok, width = events.shape
    local_heads = out_weight.shape[1] // HEAD_DIM
    seq_count = lax.axis_size("seq")
    span = seq_count // 4
    rotate = seq_count // 2
    total = tok * seq_count
    norm = float(tok * span)
    scale = 1.0 / math.sqrt(HEAD_DIM)
    grad_scale = 1.0 / math.sqrt(total)
    me = lax.axis_index("seq")
    rows = events.astype(jnp.float32)
    cent = rows - jnp.mean(rows, axis=1, keepdims=True)
    rstd = lax.rsqrt(jnp.mean(cent * cent, axis=1, keepdims=True) + EPS)
    normed = cent * rstd
    normed_b = normed.astype(jnp.bfloat16)
    proj = jnp.dot(normed_b, in_weight, preferred_element_type=jnp.float32)
    act = jax.nn.silu(proj).astype(jnp.bfloat16).reshape(tok, local_heads, 4, HEAD_DIM)
    upart = act[:, :, 0]
    values = act[:, :, 1]
    queries = act[:, :, 2]
    keys = act[:, :, 3]
    full_grad = lax.all_gather(out_grad, "head", axis=1, tiled=True)
    dout = jnp.dot(full_grad, out_weight, preferred_element_type=jnp.float32).reshape(
        tok, local_heads, HEAD_DIM
    )
    attn = saved_attn.astype(jnp.float32).reshape(tok, local_heads, HEAD_DIM)
    acent = attn - jnp.mean(attn, axis=2, keepdims=True)
    arstd = lax.rsqrt(jnp.mean(acent * acent, axis=2, keepdims=True) + EPS)
    ahat = acent * arstd
    upf = upart.astype(jnp.float32)
    gated = (ahat * upf).astype(jnp.bfloat16).reshape(tok, local_heads * HEAD_DIM)
    grad_w2 = (
        lax.dot_general(
            full_grad, gated, (((0,), (0,)), ((), ())), preferred_element_type=jnp.float32
        )
        * grad_scale
    )
    grad_u = dout * ahat
    dnorm = dout * upf
    grad_attn = (
        (
            dnorm
            - jnp.mean(dnorm, axis=2, keepdims=True)
            - ahat * jnp.mean(dnorm * ahat, axis=2, keepdims=True)
        )
        * arstd
    ).astype(jnp.bfloat16)
    offsets = jnp.arange(tok, dtype=jnp.int32)
    positions = (me + rotate) % seq_count * tok + offsets
    own_query = jnp.stack((queries, grad_attn))
    own_keys = jnp.stack((keys, values))
    grad_q, partial_value = pair_terms(
        own_query, positions, own_keys, positions, lengths, scale, norm
    )

    def carry_step(turn, state):
        visiting, carried, grad_acc = state
        visiting = shifted(visiting, "seq", 1)
        carried = shifted(carried, "seq", 1)
        key_pos = (me - turn + rotate) % seq_count * tok + offsets
        add_q, add_kv = pair_terms(own_query, positions, visiting, key_pos, lengths, scale, norm)
        return (visiting, carried + add_kv, grad_acc + add_q)

    visiting, carried, grad_q = lax.fori_loop(
        1, span + 1, carry_step, (own_keys, partial_value, grad_q)
    )
    returned = shifted(carried, "seq", -span)
    grad_k = returned[0]
    grad_v = returned[1]
    stacked = jnp.stack((grad_u, grad_v, grad_q, grad_k), axis=2)
    dproj = (
        (stacked * silu_slope(proj.reshape(tok, local_heads, 4, HEAD_DIM)))
        .astype(jnp.bfloat16)
        .reshape(tok, local_heads * 4 * HEAD_DIM)
    )
    grad_w1 = (
        lax.dot_general(
            normed_b, dproj, (((0,), (0,)), ((), ())), preferred_element_type=jnp.float32
        )
        * grad_scale
    )
    grad_w1, grad_w2 = (
        lax.psum_scatter(grad_w1, "seq", scatter_dimension=0, tiled=True),
        lax.psum_scatter(grad_w2, "seq", scatter_dimension=0, tiled=True),
    )
    partial_input = lax.dot_general(
        dproj, in_weight, (((1,), (1,)), ((), ())), preferred_element_type=jnp.float32
    )
    columns = width // lax.axis_size("head")
    first_col = lax.axis_index("head") * columns
    summed = lax.psum(partial_input, "head")
    back = (
        summed
        - jnp.mean(summed, axis=1, keepdims=True)
        - normed * jnp.mean(summed * normed, axis=1, keepdims=True)
    ) * rstd
    share = lax.dynamic_slice_in_dim(back, first_col, columns, 1)
    grad_in = (out_grad.astype(jnp.float32) + share).astype(jnp.bfloat16)
    return (grad_in, grad_w1, grad_w2)


def solution(mesh):
    return jax.shard_map(
        per_device,
        mesh=mesh,
        in_specs=(
            P("seq", None),
            P("seq", "head"),
            P("seq", "head"),
            P(None, "head"),
            P(None, "head"),
            P(),
        ),
        out_specs=(P("seq", "head"), P("seq", "head"), P("seq", "head")),
        check_vma=False,
    )
```

profile of v0, /device:TPU:1, one launch (start us, length us, event | category | flops | bytes accessed | tf_op | source)
XLA Modules:
  0.0 703.4 jit_solution(13066459899930473660)
XLA Ops:
  14.2 22.6 %all_gather.3 = bf16[256,1024]{1,0:T(8,128)(2,1)S(1)} all-gather(bf16[256,128]{1,0:T(8,128)(2,1)} %param.13), channel_id=1, replica_groups=mesh['seq'=64,'head'=8] {'head'}, dimensions={1}, use_global_device_ids=true | all-gather | bytes 589824 | tf_op jit(solution)/shard_map/all_gather | solution.py:88
  36.8 2.4 multiply_convert_fusion.1
  41.4 213.5 %while.20 = (s32[]{:T(128)}, bf16[2,256,1,128]{3,1,2,0:T(8,128)(2,1)S(1)}, f32[2,256,1,128]{3,1,2,0:T(8,128)S(1)}, f32[256,1,128]{2,0,1:T(8,128)S(1)}, s32[1,16]...) while((s32[]{:T(128)}, ...), condition=%wide.region_17.18_spmd.clone, body=%wide.region_11.17_spmd.clone.sunk | while | flops 85647376 | bytes 5777900 | solution.py:130
  41.4 9.5 %collective-permute-start = (bf16[2,256,1,128]{3,1,2,0:T(8,128)(2,1)S(1)}, bf16[2,256,1,128]{3,1,2,0:T(8,128)(2,1)S(1)}, u32[]{:S(2)}, u32[]{:S(2)}) collective-permute-start(bf16[2,256,1,128]{3,1,2,0:T(8,128)(2,1)S(1)} %get-tuple-element.519), channel_id=1, source_target_pairs={{0,8},{8,16},{16,24},{24,32},{32,40},{40,48},{48,56},{56,64},{64,7... | collective-permute-start | bytes 393224 | tf_op jit(solution)/shard_map/while/body/eval_jaxpr/ppermute | solution.py:16
  56.2 5.9 collective-permute-start
  62.1 1.9 collective-permute-start.1
  69.0 4.2 collective-permute-start
  76.8 3.3 collective-permute-done
  82.3 2.1 collective-permute-start
  84.4 2.0 collective-permute-start.1
  88.1 5.3 collective-permute-done
  93.5 2.0 collective-permute-done.1
  101.1 5.6 collective-permute-done
  106.8 2.0 collective-permute-done.1
  114.4 5.6 collective-permute-done
  120.0 2.0 collective-permute-done.1
  127.6 5.6 collective-permute-done
  133.3 2.0 collective-permute-done.1
  140.9 5.6 collective-permute-done
  146.6 2.0 collective-permute-done.1
  154.2 5.6 collective-permute-done
  159.9 2.0 collective-permute-done.1
  163.9 1.9 collective-permute-start.1
  167.5 5.6 collective-permute-done
  173.2 2.0 collective-permute-done.1
  175.2 1.9 collective-permute-start
  177.1 1.9 collective-permute-start.1
  180.8 5.6 collective-permute-done
  186.4 2.0 collective-permute-done.1
  188.5 1.9 collective-permute-start
  190.4 1.9 collective-permute-start.1
  194.0 5.6 collective-permute-done
  199.7 2.0 collective-permute-done.1
  201.8 1.9 collective-permute-start
  207.3 5.6 collective-permute-done
  213.0 2.0 collective-permute-done.1
  220.6 5.6 collective-permute-done
  226.3 2.0 collective-permute-done.1
  233.9 5.6 collective-permute-done
  239.5 2.0 collective-permute-done.1
  247.1 5.6 collective-permute-done
  252.8 2.0 collective-permute-done.1
  255.0 8.3 %collective-permute-start.2 = (f32[2,256,1,128]{1,3,2,0:T(8,128)S(1)}, f32[2,256,1,128]{1,3,2,0:T(8,128)S(1)}, u32[]{:S(2)}, u32[]{:S(2)}) collective-permute-start(f32[2,256,1,128]{1,3,2,0:T(8,128)S(1)} %copy.57), channel_id=1, source_target_pairs={{0,384},{8,392},{16,400},{24,408},{32,416},{40,424},{48,432},{56,4... | collective-permute-start | bytes 786440 | tf_op jit(solution)/shard_map/ppermute | solution.py:16
  263.4 5.6 collective-permute-done.2
  273.3 1.9 convolution_multiply_fusion.8
  275.3 88.8 %all-reduce.2.cloned.1.call-done = f32[256,1024]{1,0:T(8,128)} async-done(((f32[256,1024]{1,0:T(8,128)}), f32[256,1024]{1,0:T(8,128)}) %all-reduce.2.cloned.1.call-update) | async-done | bytes 1048592 | tf_op jit(solution)/shard_map/psum | solution.py:157
  367.4 112.1 %reduce-scatter.7.cloned.1.call-done = f32[16,128]{1,0:T(8,128)} async-done(((f32[1024,128]{1,0:T(8,128)}), f32[16,128]{1,0:T(8,128)}) %reduce-scatter.7.cloned.1.call-update) | async-done | bytes 8208
  479.5 216.4 %reduce-scatter.5.cloned.1.call-done = f32[16,512]{1,0:T(8,128)} async-done(((f32[1024,512]{1,0:T(8,128)}), f32[16,512]{1,0:T(8,128)}) %reduce-scatter.5.cloned.1.call-update) | async-done | bytes 32784 | tf_op jit(solution)/shard_map/reduce_scatter | solution.py:149
  (253 shorter events, 82.3 us)
Async XLA Ops:
  8.0 28.8 %copy-start = (bf16[1024,512]{1,0:T(8,128)(2,1)S(1)}, bf16[1024,512]{1,0:T(8,128)(2,1)}, u32[]{:S(2)}) copy-start(bf16[1024,512]{1,0:T(8,128)(2,1)} %param.15) | copy-start | bytes 3145732
  8.0 356.1 %all-reduce.2.cloned.1.call-start = ((), (), s32[]{:S(2)}) async-start(), calls=%async_computation.2 | async-start | bytes 2097152 | tf_op jit(solution)/shard_map/psum | solution.py:157
  36.8 2.6 copy-start.3
  41.4 13.1 %collective-permute-start = (bf16[2,256,1,128]{3,1,2,0:T(8,128)(2,1)S(1)}, bf16[2,256,1,128]{3,1,2,0:T(8,128)(2,1)S(1)}, u32[]{:S(2)}, u32[]{:S(2)}) collective-permute-start(bf16[2,256,1,128]{3,1,2,0:T(8,128)(2,1)S(1)} %get-tuple-element.519), channel_id=1, source_target_pairs={{0,8},{8,16},{16,24},{24,32},{32,40},{40,48},{48,56},{56,64},{64,7... | collective-permute-start | bytes 393224 | tf_op jit(solution)/shard_map/while/body/eval_jaxpr/ppermute | solution.py:16
  50.9 5.2 collective-permute-start.1
  56.2 10.7 %collective-permute-start = (bf16[2,256,1,128]{3,1,2,0:T(8,128)(2,1)S(1)}, bf16[2,256,1,128]{3,1,2,0:T(8,128)(2,1)S(1)}, u32[]{:S(2)}, u32[]{:S(2)}) collective-permute-start(bf16[2,256,1,128]{3,1,2,0:T(8,128)(2,1)S(1)} %get-tuple-element.519), channel_id=1, source_target_pairs={{0,8},{8,16},{16,24},{24,32},{32,40},{40,48},{48,56},{56,64},{64,7... | collective-permute-start | bytes 393224 | tf_op jit(solution)/shard_map/while/body/eval_jaxpr/ppermute | solution.py:16
  62.1 6.9 collective-permute-start.1
  69.0 11.1 %collective-permute-start = (bf16[2,256,1,128]{3,1,2,0:T(8,128)(2,1)S(1)}, bf16[2,256,1,128]{3,1,2,0:T(8,128)(2,1)S(1)}, u32[]{:S(2)}, u32[]{:S(2)}) collective-permute-start(bf16[2,256,1,128]{3,1,2,0:T(8,128)(2,1)S(1)} %get-tuple-element.519), channel_id=1, source_target_pairs={{0,8},{8,16},{16,24},{24,32},{32,40},{40,48},{48,56},{56,64},{64,7... | collective-permute-start | bytes 393224 | tf_op jit(solution)/shard_map/while/body/eval_jaxpr/ppermute | solution.py:16
  73.2 9.0 %collective-permute-start.1 = (f32[2,256,1,128]{3,1,2,0:T(8,128)S(1)}, f32[2,256,1,128]{3,1,2,0:T(8,128)S(1)}, u32[]{:S(2)}, u32[]{:S(2)}) collective-permute-start(f32[2,256,1,128]{3,1,2,0:T(8,128)S(1)} %get-tuple-element.520), channel_id=1, source_target_pairs={{0,8},{8,16},{16,24},{24,32},{32,40},{40,48},{48,56},{56,64},{64,7... | collective-permute-start | bytes 786440 | tf_op jit(solution)/shard_map/while/body/eval_jaxpr/ppermute | solution.py:16
  82.3 11.1 %collective-permute-start = (bf16[2,256,1,128]{3,1,2,0:T(8,128)(2,1)S(1)}, bf16[2,256,1,128]{3,1,2,0:T(8,128)(2,1)S(1)}, u32[]{:S(2)}, u32[]{:S(2)}) collective-permute-start(bf16[2,256,1,128]{3,1,2,0:T(8,128)(2,1)S(1)} %get-tuple-element.519), channel_id=1, source_target_pairs={{0,8},{8,16},{16,24},{24,32},{32,40},{40,48},{48,56},{56,64},{64,7... | collective-permute-start | bytes 393224 | tf_op jit(solution)/shard_map/while/body/eval_jaxpr/ppermute | solution.py:16
  84.4 11.1 %collective-permute-start.1 = (f32[2,256,1,128]{3,1,2,0:T(8,128)S(1)}, f32[2,256,1,128]{3,1,2,0:T(8,128)S(1)}, u32[]{:S(2)}, u32[]{:S(2)}) collective-permute-start(f32[2,256,1,128]{3,1,2,0:T(8,128)S(1)} %get-tuple-element.520), channel_id=1, source_target_pairs={{0,8},{8,16},{16,24},{24,32},{32,40},{40,48},{48,56},{56,64},{64,7... | collective-permute-start | bytes 786440 | tf_op jit(solution)/shard_map/while/body/eval_jaxpr/ppermute | solution.py:16
  95.6 11.1 %collective-permute-start = (bf16[2,256,1,128]{3,1,2,0:T(8,128)(2,1)S(1)}, bf16[2,256,1,128]{3,1,2,0:T(8,128)(2,1)S(1)}, u32[]{:S(2)}, u32[]{:S(2)}) collective-permute-start(bf16[2,256,1,128]{3,1,2,0:T(8,128)(2,1)S(1)} %get-tuple-element.519), channel_id=1, source_target_pairs={{0,8},{8,16},{16,24},{24,32},{32,40},{40,48},{48,56},{56,64},{64,7... | collective-permute-start | bytes 393224 | tf_op jit(solution)/shard_map/while/body/eval_jaxpr/ppermute | solution.py:16
  97.5 11.3 %collective-permute-start.1 = (f32[2,256,1,128]{3,1,2,0:T(8,128)S(1)}, f32[2,256,1,128]{3,1,2,0:T(8,128)S(1)}, u32[]{:S(2)}, u32[]{:S(2)}) collective-permute-start(f32[2,256,1,128]{3,1,2,0:T(8,128)S(1)} %get-tuple-element.520), channel_id=1, source_target_pairs={{0,8},{8,16},{16,24},{24,32},{32,40},{40,48},{48,56},{56,64},{64,7... | collective-permute-start | bytes 786440 | tf_op jit(solution)/shard_map/while/body/eval_jaxpr/ppermute | solution.py:16
  108.8 11.1 %collective-permute-start = (bf16[2,256,1,128]{3,1,2,0:T(8,128)(2,1)S(1)}, bf16[2,256,1,128]{3,1,2,0:T(8,128)(2,1)S(1)}, u32[]{:S(2)}, u32[]{:S(2)}) collective-permute-start(bf16[2,256,1,128]{3,1,2,0:T(8,128)(2,1)S(1)} %get-tuple-element.519), channel_id=1, source_target_pairs={{0,8},{8,16},{16,24},{24,32},{32,40},{40,48},{48,56},{56,64},{64,7... | collective-permute-start | bytes 393224 | tf_op jit(solution)/shard_map/while/body/eval_jaxpr/ppermute | solution.py:16
  110.8 11.3 %collective-permute-start.1 = (f32[2,256,1,128]{3,1,2,0:T(8,128)S(1)}, f32[2,256,1,128]{3,1,2,0:T(8,128)S(1)}, u32[]{:S(2)}, u32[]{:S(2)}) collective-permute-start(f32[2,256,1,128]{3,1,2,0:T(8,128)S(1)} %get-tuple-element.520), channel_id=1, source_target_pairs={{0,8},{8,16},{16,24},{24,32},{32,40},{40,48},{48,56},{56,64},{64,7... | collective-permute-start | bytes 786440 | tf_op jit(solution)/shard_map/while/body/eval_jaxpr/ppermute | solution.py:16
  122.1 11.1 %collective-permute-start = (bf16[2,256,1,128]{3,1,2,0:T(8,128)(2,1)S(1)}, bf16[2,256,1,128]{3,1,2,0:T(8,128)(2,1)S(1)}, u32[]{:S(2)}, u32[]{:S(2)}) collective-permute-start(bf16[2,256,1,128]{3,1,2,0:T(8,128)(2,1)S(1)} %get-tuple-element.519), channel_id=1, source_target_pairs={{0,8},{8,16},{16,24},{24,32},{32,40},{40,48},{48,56},{56,64},{64,7... | collective-permute-start | bytes 393224 | tf_op jit(solution)/shard_map/while/body/eval_jaxpr/ppermute | solution.py:16
  124.0 11.3 %collective-permute-start.1 = (f32[2,256,1,128]{3,1,2,0:T(8,128)S(1)}, f32[2,256,1,128]{3,1,2,0:T(8,128)S(1)}, u32[]{:S(2)}, u32[]{:S(2)}) collective-permute-start(f32[2,256,1,128]{3,1,2,0:T(8,128)S(1)} %get-tuple-element.520), channel_id=1, source_target_pairs={{0,8},{8,16},{16,24},{24,32},{32,40},{40,48},{48,56},{56,64},{64,7... | collective-permute-start | bytes 786440 | tf_op jit(solution)/shard_map/while/body/eval_jaxpr/ppermute | solution.py:16
  135.4 11.1 %collective-permute-start = (bf16[2,256,1,128]{3,1,2,0:T(8,128)(2,1)S(1)}, bf16[2,256,1,128]{3,1,2,0:T(8,128)(2,1)S(1)}, u32[]{:S(2)}, u32[]{:S(2)}) collective-permute-start(bf16[2,256,1,128]{3,1,2,0:T(8,128)(2,1)S(1)} %get-tuple-element.519), channel_id=1, source_target_pairs={{0,8},{8,16},{16,24},{24,32},{32,40},{40,48},{48,56},{56,64},{64,7... | collective-permute-start | bytes 393224 | tf_op jit(solution)/shard_map/while/body/eval_jaxpr/ppermute | solution.py:16
  137.3 11.3 %collective-permute-start.1 = (f32[2,256,1,128]{3,1,2,0:T(8,128)S(1)}, f32[2,256,1,128]{3,1,2,0:T(8,128)S(1)}, u32[]{:S(2)}, u32[]{:S(2)}) collective-permute-start(f32[2,256,1,128]{3,1,2,0:T(8,128)S(1)} %get-tuple-element.520), channel_id=1, source_target_pairs={{0,8},{8,16},{16,24},{24,32},{32,40},{40,48},{48,56},{56,64},{64,7... | collective-permute-start | bytes 786440 | tf_op jit(solution)/shard_map/while/body/eval_jaxpr/ppermute | solution.py:16
  148.7 11.1 %collective-permute-start = (bf16[2,256,1,128]{3,1,2,0:T(8,128)(2,1)S(1)}, bf16[2,256,1,128]{3,1,2,0:T(8,128)(2,1)S(1)}, u32[]{:S(2)}, u32[]{:S(2)}) collective-permute-start(bf16[2,256,1,128]{3,1,2,0:T(8,128)(2,1)S(1)} %get-tuple-element.519), channel_id=1, source_target_pairs={{0,8},{8,16},{16,24},{24,32},{32,40},{40,48},{48,56},{56,64},{64,7... | collective-permute-start | bytes 393224 | tf_op jit(solution)/shard_map/while/body/eval_jaxpr/ppermute | solution.py:16
  150.6 11.3 %collective-permute-start.1 = (f32[2,256,1,128]{3,1,2,0:T(8,128)S(1)}, f32[2,256,1,128]{3,1,2,0:T(8,128)S(1)}, u32[]{:S(2)}, u32[]{:S(2)}) collective-permute-start(f32[2,256,1,128]{3,1,2,0:T(8,128)S(1)} %get-tuple-element.520), channel_id=1, source_target_pairs={{0,8},{8,16},{16,24},{24,32},{32,40},{40,48},{48,56},{56,64},{64,7... | collective-permute-start | bytes 786440 | tf_op jit(solution)/shard_map/while/body/eval_jaxpr/ppermute | solution.py:16
  161.9 11.1 %collective-permute-start = (bf16[2,256,1,128]{3,1,2,0:T(8,128)(2,1)S(1)}, bf16[2,256,1,128]{3,1,2,0:T(8,128)(2,1)S(1)}, u32[]{:S(2)}, u32[]{:S(2)}) collective-permute-start(bf16[2,256,1,128]{3,1,2,0:T(8,128)(2,1)S(1)} %get-tuple-element.519), channel_id=1, source_target_pairs={{0,8},{8,16},{16,24},{24,32},{32,40},{40,48},{48,56},{56,64},{64,7... | collective-permute-start | bytes 393224 | tf_op jit(solution)/shard_map/while/body/eval_jaxpr/ppermute | solution.py:16
  163.9 11.3 %collective-permute-start.1 = (f32[2,256,1,128]{3,1,2,0:T(8,128)S(1)}, f32[2,256,1,128]{3,1,2,0:T(8,128)S(1)}, u32[]{:S(2)}, u32[]{:S(2)}) collective-permute-start(f32[2,256,1,128]{3,1,2,0:T(8,128)S(1)} %get-tuple-element.520), channel_id=1, source_target_pairs={{0,8},{8,16},{16,24},{24,32},{32,40},{40,48},{48,56},{56,64},{64,7... | collective-permute-start | bytes 786440 | tf_op jit(solution)/shard_map/while/body/eval_jaxpr/ppermute | solution.py:16
  175.2 11.1 %collective-permute-start = (bf16[2,256,1,128]{3,1,2,0:T(8,128)(2,1)S(1)}, bf16[2,256,1,128]{3,1,2,0:T(8,128)(2,1)S(1)}, u32[]{:S(2)}, u32[]{:S(2)}) collective-permute-start(bf16[2,256,1,128]{3,1,2,0:T(8,128)(2,1)S(1)} %get-tuple-element.519), channel_id=1, source_target_pairs={{0,8},{8,16},{16,24},{24,32},{32,40},{40,48},{48,56},{56,64},{64,7... | collective-permute-start | bytes 393224 | tf_op jit(solution)/shard_map/while/body/eval_jaxpr/ppermute | solution.py:16
  177.1 11.3 %collective-permute-start.1 = (f32[2,256,1,128]{3,1,2,0:T(8,128)S(1)}, f32[2,256,1,128]{3,1,2,0:T(8,128)S(1)}, u32[]{:S(2)}, u32[]{:S(2)}) collective-permute-start(f32[2,256,1,128]{3,1,2,0:T(8,128)S(1)} %get-tuple-element.520), channel_id=1, source_target_pairs={{0,8},{8,16},{16,24},{24,32},{32,40},{40,48},{48,56},{56,64},{64,7... | collective-permute-start | bytes 786440 | tf_op jit(solution)/shard_map/while/body/eval_jaxpr/ppermute | solution.py:16
  188.5 11.1 %collective-permute-start = (bf16[2,256,1,128]{3,1,2,0:T(8,128)(2,1)S(1)}, bf16[2,256,1,128]{3,1,2,0:T(8,128)(2,1)S(1)}, u32[]{:S(2)}, u32[]{:S(2)}) collective-permute-start(bf16[2,256,1,128]{3,1,2,0:T(8,128)(2,1)S(1)} %get-tuple-element.519), channel_id=1, source_target_pairs={{0,8},{8,16},{16,24},{24,32},{32,40},{40,48},{48,56},{56,64},{64,7... | collective-permute-start | bytes 393224 | tf_op jit(solution)/shard_map/while/body/eval_jaxpr/ppermute | solution.py:16
  190.4 11.3 %collective-permute-start.1 = (f32[2,256,1,128]{3,1,2,0:T(8,128)S(1)}, f32[2,256,1,128]{3,1,2,0:T(8,128)S(1)}, u32[]{:S(2)}, u32[]{:S(2)}) collective-permute-start(f32[2,256,1,128]{3,1,2,0:T(8,128)S(1)} %get-tuple-element.520), channel_id=1, source_target_pairs={{0,8},{8,16},{16,24},{24,32},{32,40},{40,48},{48,56},{56,64},{64,7... | collective-permute-start | bytes 786440 | tf_op jit(solution)/shard_map/while/body/eval_jaxpr/ppermute | solution.py:16
  201.8 11.1 %collective-permute-start = (bf16[2,256,1,128]{3,1,2,0:T(8,128)(2,1)S(1)}, bf16[2,256,1,128]{3,1,2,0:T(8,128)(2,1)S(1)}, u32[]{:S(2)}, u32[]{:S(2)}) collective-permute-start(bf16[2,256,1,128]{3,1,2,0:T(8,128)(2,1)S(1)} %get-tuple-element.519), channel_id=1, source_target_pairs={{0,8},{8,16},{16,24},{24,32},{32,40},{40,48},{48,56},{56,64},{64,7... | collective-permute-start | bytes 393224 | tf_op jit(solution)/shard_map/while/body/eval_jaxpr/ppermute | solution.py:16
  203.7 11.3 %collective-permute-start.1 = (f32[2,256,1,128]{3,1,2,0:T(8,128)S(1)}, f32[2,256,1,128]{3,1,2,0:T(8,128)S(1)}, u32[]{:S(2)}, u32[]{:S(2)}) collective-permute-start(f32[2,256,1,128]{3,1,2,0:T(8,128)S(1)} %get-tuple-element.520), channel_id=1, source_target_pairs={{0,8},{8,16},{16,24},{24,32},{32,40},{40,48},{48,56},{56,64},{64,7... | collective-permute-start | bytes 786440 | tf_op jit(solution)/shard_map/while/body/eval_jaxpr/ppermute | solution.py:16
  215.0 11.1 %collective-permute-start = (bf16[2,256,1,128]{3,1,2,0:T(8,128)(2,1)S(1)}, bf16[2,256,1,128]{3,1,2,0:T(8,128)(2,1)S(1)}, u32[]{:S(2)}, u32[]{:S(2)}) collective-permute-start(bf16[2,256,1,128]{3,1,2,0:T(8,128)(2,1)S(1)} %get-tuple-element.519), channel_id=1, source_target_pairs={{0,8},{8,16},{16,24},{24,32},{32,40},{40,48},{48,56},{56,64},{64,7... | collective-permute-start | bytes 393224 | tf_op jit(solution)/shard_map/while/body/eval_jaxpr/ppermute | solution.py:16
  217.0 11.3 %collective-permute-start.1 = (f32[2,256,1,128]{3,1,2,0:T(8,128)S(1)}, f32[2,256,1,128]{3,1,2,0:T(8,128)S(1)}, u32[]{:S(2)}, u32[]{:S(2)}) collective-permute-start(f32[2,256,1,128]{3,1,2,0:T(8,128)S(1)} %get-tuple-element.520), channel_id=1, source_target_pairs={{0,8},{8,16},{16,24},{24,32},{32,40},{40,48},{48,56},{56,64},{64,7... | collective-permute-start | bytes 786440 | tf_op jit(solution)/shard_map/while/body/eval_jaxpr/ppermute | solution.py:16
  228.3 11.1 %collective-permute-start = (bf16[2,256,1,128]{3,1,2,0:T(8,128)(2,1)S(1)}, bf16[2,256,1,128]{3,1,2,0:T(8,128)(2,1)S(1)}, u32[]{:S(2)}, u32[]{:S(2)}) collective-permute-start(bf16[2,256,1,128]{3,1,2,0:T(8,128)(2,1)S(1)} %get-tuple-element.519), channel_id=1, source_target_pairs={{0,8},{8,16},{16,24},{24,32},{32,40},{40,48},{48,56},{56,64},{64,7... | collective-permute-start | bytes 393224 | tf_op jit(solution)/shard_map/while/body/eval_jaxpr/ppermute | solution.py:16
  230.2 11.3 %collective-permute-start.1 = (f32[2,256,1,128]{3,1,2,0:T(8,128)S(1)}, f32[2,256,1,128]{3,1,2,0:T(8,128)S(1)}, u32[]{:S(2)}, u32[]{:S(2)}) collective-permute-start(f32[2,256,1,128]{3,1,2,0:T(8,128)S(1)} %get-tuple-element.520), channel_id=1, source_target_pairs={{0,8},{8,16},{16,24},{24,32},{32,40},{40,48},{48,56},{56,64},{64,7... | collective-permute-start | bytes 786440 | tf_op jit(solution)/shard_map/while/body/eval_jaxpr/ppermute | solution.py:16
  241.6 11.1 %collective-permute-start = (bf16[2,256,1,128]{3,1,2,0:T(8,128)(2,1)S(1)}, bf16[2,256,1,128]{3,1,2,0:T(8,128)(2,1)S(1)}, u32[]{:S(2)}, u32[]{:S(2)}) collective-permute-start(bf16[2,256,1,128]{3,1,2,0:T(8,128)(2,1)S(1)} %get-tuple-element.519), channel_id=1, source_target_pairs={{0,8},{8,16},{16,24},{24,32},{32,40},{40,48},{48,56},{56,64},{64,7... | collective-permute-start | bytes 393224 | tf_op jit(solution)/shard_map/while/body/eval_jaxpr/ppermute | solution.py:16
  243.5 11.3 %collective-permute-start.1 = (f32[2,256,1,128]{3,1,2,0:T(8,128)S(1)}, f32[2,256,1,128]{3,1,2,0:T(8,128)S(1)}, u32[]{:S(2)}, u32[]{:S(2)}) collective-permute-start(f32[2,256,1,128]{3,1,2,0:T(8,128)S(1)} %get-tuple-element.520), channel_id=1, source_target_pairs={{0,8},{8,16},{16,24},{24,32},{32,40},{40,48},{48,56},{56,64},{64,7... | collective-permute-start | bytes 786440 | tf_op jit(solution)/shard_map/while/body/eval_jaxpr/ppermute | solution.py:16
  255.0 14.0 %collective-permute-start.2 = (f32[2,256,1,128]{1,3,2,0:T(8,128)S(1)}, f32[2,256,1,128]{1,3,2,0:T(8,128)S(1)}, u32[]{:S(2)}, u32[]{:S(2)}) collective-permute-start(f32[2,256,1,128]{1,3,2,0:T(8,128)S(1)} %copy.57), channel_id=1, source_target_pairs={{0,384},{8,392},{16,400},{24,408},{32,416},{40,424},{48,432},{56,4... | collective-permute-start | bytes 786440 | tf_op jit(solution)/shard_map/ppermute | solution.py:16
  271.9 1.4 copy-start.1
  272.0 207.6 %reduce-scatter.7.cloned.1.call-start = ((), (), s32[]{:S(2)}) async-start(), calls=%async_computation.4 | async-start | bytes 532480
  273.3 422.7 %reduce-scatter.5.cloned.1.call-start = ((), (), s32[]{:S(2)}) async-start(), calls=%async_computation.3 | async-start | bytes 2129920 | tf_op jit(solution)/shard_map/reduce_scatter | solution.py:149
  275.3 90.4 %copy-start.2 = (bf16[256,128]{1,0:T(8,128)(2,1)S(1)}, bf16[256,128]{1,0:T(8,128)(2,1)}, u32[]{:S(2)}) copy-start(bf16[256,128]{1,0:T(8,128)(2,1)} %param.13) | copy-start | bytes 196612
Sparse Core Ops, SparseCore 0:
  272.1 91.9 all-reduce.1
Sparse Core Ops, SparseCore 1:
  277.6 201.9 reduce-scatter.6
  484.6 211.3 reduce-scatter.4
where the time goes:
time: 716 us; the launch traced here: 703 us
  waiting for transfers between devices  528 us (74%)
  starting transfers between devices  84 us (12%)
  other arithmetic  25.3 us (4%)
  blocking collectives  22.6 us (3%)
  between operations  16.4 us (2%)
  loops' own time  13 us (2%)
  matrix products  10.7 us (1%)
    reduce_scatter x1, waiting for transfers between devices, per_device(): lax.psum_scatter(grad_w1, 'seq', scatter_dimension=0, tiled=True)  216 us
    unnamed x4, waiting for transfers between devices  112 us
    ppermute x33, waiting for transfers between devices, shifted(): lax.ppermute(x, axis, [(i, (i + by) % devices) for i in range(devices)])  111 us
    psum x1, waiting for transfers between devices, per_device(): summed = lax.psum(partial_input, 'head')  88.8 us
    ppermute x33, starting transfers between devices, shifted(): lax.ppermute(x, axis, [(i, (i + by) % devices) for i in range(devices)])  83.8 us
    all_gather x1, blocking collectives, per_device(): full_grad = lax.all_gather(out_grad, 'head', axis=1, tiled=True)  22.6 us
  transfers between devices with their start and end apart: 36, of which 35 were waited for; matrix products, arithmetic and copies ran while one was open for 4% of the time, Pallas kernels for 0%

commit v1 on v0

v1 whole, which is shorter than its diff:
```python
import math

import jax
import jax.numpy as jnp
from jax import lax
from jax.experimental import pallas as pl
from jax.experimental.pallas import tpu as pltpu
from jax.sharding import PartitionSpec as P

HEADS = 8
HD = 128
TOK = 256
WIDTH = 1024
PLANES = 16
NSEQ = 16
REACH = 4
MOST = 4096.0
EPS = 1e-05
SCALE = 1.0 / math.sqrt(HD)
GRAD_SCALE = 1.0 / 128.0
MESH = pl.DeviceIdType.MESH
F32 = jnp.float32
BF16 = jnp.bfloat16
NEAR_LAST = (8, 7, 9, 6, 10, 5, 11, 4, 12, 3, 13, 2, 14, 1, 15)


def nn(a, b):
    return jnp.dot(a, b, preferred_element_type=F32)


def nt(a, b):
    return lax.dot_general(a, b, (((1,), (1,)), ((), ())), preferred_element_type=F32)


def tn(a, b):
    return lax.dot_general(a, b, (((0,), (0,)), ((), ())), preferred_element_type=F32)


def push(src, dst, sent, came, device):
    return pltpu.make_async_remote_copy(
        src_ref=src,
        dst_ref=dst,
        send_sem=sent,
        recv_sem=came,
        device_id=device,
        device_id_type=MESH,
    )


def kernel(
    ev, og, sa, wi, wo, lens, gi, g1, g2,
    n8, nb, ntr, rsd, slope, upart, ahat_s, arstd_s, dproj,
    fg, qa, doa, kva, kvg, dqs, dqr,
    kvs1, kvr1, kvs2, kvr2,
    ge, ge1, ga1, ge2, ga2, ge3,
    gl, gl1, gb1, gl2, gb2, gl3,
    ps, pr, own, st, sr,
    fg_s, fg_r, q_s, q_r, do_s, do_r, kv_s, kv_r, dq_s, dq_r, kx_s, kx_r,
    e12_s, e12_r, e3_s, e3_r, l12_s, l12_r, l3_s, l3_r, p_s, p_r, t_s, t_r,
):
    s = lax.axis_index("seq")
    h = lax.axis_index("head")
    z = s // 4
    xh = (s // 2) % 2
    c = s % 2

    def at_z(i):
        return (((z + i) % PLANES) * 4 + xh * 2 + c, h)

    def in_plane(i):
        return (z * 4 + ((xh + i // 2) % 2) * 2 + (c + i % 2) % 2, h)

    def at_head(i):
        return (s, (h + i) % HEADS)

    barrier = pltpu.get_barrier_semaphore()
    for i in range(1, HEADS):
        pl.semaphore_signal(barrier, inc=1, device_id=at_head(i), device_id_type=MESH)
    for i in range(1, 4):
        pl.semaphore_signal(barrier, inc=1, device_id=in_plane(i), device_id_type=MESH)
    for i in range(1, PLANES):
        pl.semaphore_signal(barrier, inc=1, device_id=at_z(i), device_id_type=MESH)

    def norm_rows(i, carry):
        r = pl.multiple_of(i * 32, 32)
        x = ev[pl.ds(r, 32), :].astype(F32)
        cent = x - jnp.mean(x, axis=1, keepdims=True)
        rstd = lax.rsqrt(jnp.mean(cent * cent, axis=1, keepdims=True) + EPS)
        normed = cent * rstd
        nb[pl.ds(r, 32), :] = normed.astype(BF16)
        for j in range(HEADS):
            n8[j, pl.ds(r, 32), :] = normed[:, j * HD : (j + 1) * HD]
        rsd[pl.ds(r, 32), :] = jnp.broadcast_to(rstd, (32, HD))
        return carry

    lax.fori_loop(0, TOK // 32, norm_rows, 0)

    pl.semaphore_wait(barrier, HEADS - 1 + 3 + PLANES - 1)
    fg_copies = [
        push(og, fg.at[i], fg_s.at[i], fg_r.at[i], at_head(i)) for i in range(1, HEADS)
    ]
    for copy in fg_copies:
        copy.start()

    for part in (2, 3, 1, 0):
        proj = nn(nb[...], wi[:, part * HD : (part + 1) * HD])
        sig = 0.5 * jnp.tanh(0.5 * proj) + 0.5
        act = (proj * sig).astype(BF16)
        slope[part] = sig * (1.0 + proj * (1.0 - sig))
        if part == 0:
            upart[...] = act.astype(F32)
        elif part == 1:
            kva[0, 1] = act
        elif part == 2:
            qa[0] = act
        else:
            kva[0, 0] = act

    q_copies = [
        push(qa.at[0], qa.at[d], q_s.at[d], q_r.at[d], at_z(PLANES - d))
        for d in range(REACH, 0, -1)
    ]
    kv_copies = [
        push(kva.at[0], kva.at[i], kv_s.at[i], kv_r.at[i], in_plane(i)) for i in (3, 2, 1)
    ]
    for copy in kv_copies + q_copies:
        copy.start()

    attn = sa[...].astype(F32)
    cent = attn - jnp.mean(attn, axis=1, keepdims=True)
    arstd = lax.rsqrt(jnp.mean(cent * cent, axis=1, keepdims=True) + EPS)
    ahat_s[...] = cent * arstd
    arstd_s[...] = jnp.broadcast_to(arstd, (TOK, HD))
    kvg[...] = jnp.zeros_like(kvg)

    def turn_columns(j, carry):
        ntr[pl.ds(pl.multiple_of(j * HD, HD), HD), :] = n8[j].T.astype(BF16)
        return carry

    lax.fori_loop(0, HEADS, turn_columns, 0)

    dout = nn(og[...], wo[pl.ds(pl.multiple_of(h * HD, HD), HD), :])
    for i in range(1, HEADS):
        fg_copies[i - 1].wait_recv()
        row = pl.multiple_of(((h + HEADS - i) % HEADS) * HD, HD)
        dout += nn(fg[i], wo[pl.ds(row, HD), :])
    ahat = ahat_s[...]
    dnorm = dout * upart[...]
    doa[0] = (
        (
            dnorm
            - jnp.mean(dnorm, axis=1, keepdims=True)
            - ahat * jnp.mean(dnorm * ahat, axis=1, keepdims=True)
        )
        * arstd_s[...]
    ).astype(BF16)
    do_copies = [
        push(doa.at[0], doa.at[d], do_s.at[d], do_r.at[d], at_z(PLANES - d))
        for d in range(REACH, 0, -1)
    ]
    for copy in do_copies:
        copy.start()

    dproj[:, 0:HD] = (dout * ahat * slope[0]).astype(BF16)
    gated = (ahat * upart[...]).astype(BF16)
    ge[:, :, :, 0:HD] = (nn(ntr[...], dproj[:, 0:HD])).astype(BF16).reshape(32, 2, 16, HD)
    for i in range(HEADS):
        block = pl.ds(((h + HEADS - i) % HEADS) * 4, 4)
        rows = og[...] if i == 0 else fg[i]
        ge[block, :, :, HD : 2 * HD] = tn(rows, gated).astype(BF16).reshape(4, 2, 16, HD)

    def sum_parts(whole, into, over):
        one = push(whole.at[:, 1 - c], into, over[0].at[0], over[1].at[0], in_plane(1))
        return one

    def add_first(whole, came, kept):
        def step(i, carry):
            kept[i] = (
                whole[pl.ds(2 * i, 2), c].astype(F32) + came[pl.ds(2 * i, 2)].astype(F32)
            ).astype(BF16)
            return carry

        lax.fori_loop(0, PLANES, step, 0)

    def sum_across(kept, into, over):
        return push(kept.at[:, 1 - xh], into, over[0].at[1], over[1].at[1], in_plane(2))

    def add_second(kept, came, final):
        def step(i, carry):
            final[i] = (kept[i, xh].astype(F32) + came[i].astype(F32)).astype(BF16)
            return carry

        lax.fori_loop(0, PLANES, step, 0)

    def sum_planes(final, into, over):
        return [
            push(final.at[(z + i) % PLANES], into.at[i], over[0].at[i], over[1].at[i], at_z(i))
            for i in NEAR_LAST
        ]

    def add_third(final, came):
        total = final[z].astype(F32)
        for i in range(1, PLANES):
            total += came[i].astype(F32)
        return total * GRAD_SCALE

    e_first = sum_parts(ge, ge1, (e12_s, e12_r))
    e_first.start()

    ends = []
    run = 0
    for i in range(NSEQ):
        run = run + lens[i]
        ends.append(run)
    own_plane = (z + PLANES // 2) % PLANES

    for copy in kv_copies:
        copy.wait_recv()

    def attend(turn, carry):
        d = jnp.where(turn == 0, 0, REACH + 1 - turn)

        @pl.when(turn > 0)
        def _():
            push(qa.at[0], qa.at[d], q_s.at[d], q_r.at[d], at_z(d)).wait_recv()
            push(doa.at[0], doa.at[d], do_s.at[d], do_r.at[d], at_z(d)).wait_recv()

        queries = qa[d]
        upstream = doa[d]
        lane = lax.broadcasted_iota(jnp.int32, (1, TOK), 1)
        qpos = ((own_plane + d) % PLANES) * 1024 + xh * 512 + c * 256 + lane
        first = jnp.zeros((1, TOK), jnp.int32)
        for end in ends:
            first = jnp.maximum(first, jnp.where(qpos >= end, end, 0))

        def block(i, grad_q):
            keys = kva[i, 0]
            values = kva[i, 1]
            kpos = (
                own_plane * 1024
                + ((xh + i // 2) % 2) * 512
                + ((c + i) % 2) * 256
                + lax.broadcasted_iota(jnp.int32, (TOK, TOK), 0)
            )
            mask = (kpos <= qpos) & (kpos >= first)
            scores = nt(keys, queries) * SCALE
            sig = 0.5 * jnp.tanh(0.5 * scores) + 0.5
            weight = scores * sig
            dprob = nt(values, upstream)
            dscore = jnp.where(mask, dprob * (sig + weight * (1.0 - sig)), 0.0).astype(BF16)
            weight = jnp.where(mask, weight, 0.0).astype(BF16)
            kvg[i, 0] += nn(dscore, queries)
            kvg[i, 1] += nn(weight, upstream)
            return grad_q + tn(dscore, keys)

        grad_q = lax.fori_loop(0, 4, block, jnp.zeros((TOK, HD), F32))
        dqs[d] = grad_q.astype(BF16)

        @pl.when(turn > 0)
        def _():
            push(dqs.at[d], dqr.at[d], dq_s.at[d], dq_r.at[d], at_z(d)).start()

        return carry

    lax.fori_loop(0, REACH + 1, attend, 0)

    for j in range(2):
        other = 2 * j + 1
        kvs1[j] = kvg[other].astype(BF16)
    k_first = push(kvs1, kvr1, kx_s.at[0], kx_r.at[0], in_plane(1))
    k_first.start()

    e_first.wait_recv()
    add_first(ge, ge1, ga1)
    e_second = sum_across(ga1, ge2, (e12_s, e12_r))
    e_second.start()

    k_first.wait_recv()
    kvs2[...] = (kvg[2] + kvr1[1].astype(F32)).astype(BF16)
    k_second = push(kvs2, kvr2, kx_s.at[1], kx_r.at[1], in_plane(2))
    k_second.start()

    dq_copies = [
        push(dqs.at[d], dqr.at[d], dq_s.at[d], dq_r.at[d], at_z(d)) for d in range(1, REACH + 1)
    ]
    grad_q = dqs[0].astype(F32)
    for d in range(REACH, 0, -1):
        dq_copies[d - 1].wait_recv()
        grad_q += dqr[d].astype(F32)
    dproj[:, 2 * HD : 3 * HD] = (grad_q * (SCALE / MOST) * slope[2]).astype(BF16)
    gl[:, :, :, HD : 2 * HD] = (
        nn(ntr[...], dproj[:, 2 * HD : 3 * HD]).astype(BF16).reshape(32, 2, 16, HD)
    )

    e_second.wait_recv()
    add_second(ga1, ge2, ga2)
    e_third = sum_planes(ga2, ge3, (e3_s, e3_r))
    for copy in e_third:
        copy.start()

    k_second.wait_recv()
    grad_k = kvg[0, 0] + kvr1[0, 0].astype(F32) + kvr2[0].astype(F32)
    grad_v = kvg[0, 1] + kvr1[0, 1].astype(F32) + kvr2[1].astype(F32)
    dproj[:, 3 * HD :] = (grad_k * (SCALE / MOST) * slope[3]).astype(BF16)
    dproj[:, HD : 2 * HD] = (grad_v * (1.0 / MOST) * slope[1]).astype(BF16)
    gl[:, :, :, 2 * HD :] = nn(ntr[...], dproj[:, 3 * HD :]).astype(BF16).reshape(32, 2, 16, HD)
    gl[:, :, :, 0:HD] = nn(ntr[...], dproj[:, HD : 2 * HD]).astype(BF16).reshape(32, 2, 16, HD)
    l_first = sum_parts(gl, gl1, (l12_s, l12_r))
    l_first.start()

    total = jnp.zeros((TOK, HD), F32)
    along = jnp.zeros((TOK, HD), F32)
    p_copies = []
    for i in (6, 2, 7, 5, 3, 1, 4, 0):
        hh = (h + i) % HEADS
        part = nt(dproj[...], wi[pl.ds(pl.multiple_of(hh * HD, HD), HD), :])
        total += part
        along += part * n8[hh]
        if i:
            ps[i] = part.astype(BF16)
            copy = push(ps.at[i], pr.at[i], p_s.at[i], p_r.at[i], at_head(i))
            copy.start()
            p_copies.append((i, copy))
        else:
            own[...] = part
    lane = lax.broadcasted_iota(jnp.int32, (TOK, HD), 1)
    both = jnp.where(
        lane == 0,
        jnp.sum(total, axis=1, keepdims=True),
        jnp.where(lane == 1, jnp.sum(along, axis=1, keepdims=True), 0.0),
    )
    st[...] = both.T[0:8, :]
    t_copies = [
        push(st, sr.at[i], t_s.at[i], t_r.at[i], at_head(i)) for i in range(1, HEADS)
    ]
    for copy in t_copies:
        copy.start()

    l_first.wait_recv()
    add_first(gl, gl1, gb1)
    l_second = sum_across(gb1, gl2, (l12_s, l12_r))
    l_second.start()

    for copy in e_third:
        copy.wait_recv()
    early = add_third(ga2, ge3)
    g1[:, 0:HD] = early[:, 0:HD]
    g2[...] = early[:, HD:]

    l_second.wait_recv()
    add_second(gb1, gl2, gb2)
    l_third = sum_planes(gb2, gl3, (l3_s, l3_r))
    for copy in l_third:
        copy.start()

    summed = own[...]
    for i, copy in p_copies:
        copy.wait_recv()
        summed += pr[i].astype(F32)
    stats = st[...]
    for i in range(1, HEADS):
        t_copies[i - 1].wait_recv()
        stats += sr[i]
    wide = jnp.concatenate([stats, jnp.zeros((HD - 8, TOK), F32)], axis=0).T * (1.0 / WIDTH)
    back = (summed - wide[:, 0:1] - n8[h] * wide[:, 1:2]) * rsd[...]
    gi[...] = (og[...].astype(F32) + back).astype(BF16)

    for copy in l_third:
        copy.wait_recv()
    late = add_third(gb2, gl3)
    g1[:, HD:] = late

    for copy in (
        fg_copies + q_copies + kv_copies + do_copies + dq_copies + e_third + l_third + t_copies
    ):
        copy.wait_send()
    for i, copy in p_copies:
        copy.wait_send()
    for copy in (e_first, e_second, k_first, k_second, l_first, l_second):
        copy.wait_send()


def rows_of(columns):
    return [
        pltpu.VMEM((32, 2, 16, columns), BF16),
        pltpu.VMEM((32, 16, columns), BF16),
        pltpu.VMEM((16, 2, 16, columns), BF16),
        pltpu.VMEM((16, 16, columns), BF16),
        pltpu.VMEM((16, 16, columns), BF16),
        pltpu.VMEM((16, 16, columns), BF16),
    ]


def per_device(events, out_grad, saved_attn, in_weight, out_weight, lengths):
    tile = (TOK, HD)
    vmem = pl.BlockSpec(memory_space=pltpu.VMEM)
    dma = pltpu.SemaphoreType.DMA
    scratch = [
        pltpu.VMEM((HEADS,) + tile, F32),
        pltpu.VMEM((TOK, WIDTH), BF16),
        pltpu.VMEM((WIDTH, TOK), BF16),
        pltpu.VMEM(tile, F32),
        pltpu.VMEM((4,) + tile, F32),
        pltpu.VMEM(tile, F32),
        pltpu.VMEM(tile, F32),
        pltpu.VMEM(tile, F32),
        pltpu.VMEM((TOK, 4 * HD), BF16),
        pltpu.VMEM((HEADS,) + tile, BF16),
        pltpu.VMEM((REACH + 1,) + tile, BF16),
        pltpu.VMEM((REACH + 1,) + tile, BF16),
        pltpu.VMEM((4, 2) + tile, BF16),
        pltpu.VMEM((4, 2) + tile, F32),
        pltpu.VMEM((REACH + 1,) + tile, BF16),
        pltpu.VMEM((REACH + 1,) + tile, BF16),
        pltpu.VMEM((2, 2) + tile, BF16),
        pltpu.VMEM((2, 2) + tile, BF16),
        pltpu.VMEM((2,) + tile, BF16),
        pltpu.VMEM((2,) + tile, BF16),
        *rows_of(2 * HD),
        *rows_of(3 * HD),
        pltpu.VMEM((HEADS,) + tile, BF16),
        pltpu.VMEM((HEADS,) + tile, BF16),
        pltpu.VMEM(tile, F32),
        pltpu.VMEM((8, TOK), F32),
        pltpu.VMEM((HEADS, 8, TOK), F32),
    ]
    counts = (8, 8, 5, 5, 5, 5, 4, 4, 5, 5, 2, 2, 2, 2, 16, 16, 2, 2, 16, 16, 8, 8, 8, 8)
    scratch += [dma((n,)) for n in counts]
    return pl.pallas_call(
        kernel,
        out_shape=(
            jax.ShapeDtypeStruct(tile, BF16),
            jax.ShapeDtypeStruct((16, 4 * HD), F32),
            jax.ShapeDtypeStruct((16, HD), F32),
        ),
        in_specs=[vmem] * 5 + [pl.BlockSpec(memory_space=pltpu.SMEM)],
        out_specs=(vmem,) * 3,
        scratch_shapes=scratch,
        compiler_params=pltpu.CompilerParams(
            collective_id=0, has_side_effects=True, vmem_limit_bytes=48 * 2**20
        ),
        name="layer_backward",
    )(events, out_grad, saved_attn, in_weight, out_weight, lengths)


def solution(mesh):
    return jax.shard_map(
        per_device,
        mesh=mesh,
        in_specs=(
            P("seq", None),
            P("seq", "head"),
            P("seq", "head"),
            P(None, "head"),
            P(None, "head"),
            P(),
        ),
        out_specs=(P("seq", "head"), P("seq", "head"), P("seq", "head")),
        check_vma=False,
    )
```

time: 716 us -> 92 us (0.13); the launches traced: 703 us -> 90.3 us
  waiting for transfers between devices: 528 us -> 0 us
  starting transfers between devices: 84 us -> 0 us
  Pallas kernels: 0 us -> 82.3 us
  other arithmetic: 25.3 us -> 0 us
  blocking collectives: 22.6 us -> 0 us
  between operations: 16.4 us -> 0.65 us
  loops' own time: 13 us -> 0 us
  matrix products: 10.7 us -> 0 us
    reduce_scatter x1 -> x0, waiting for transfers between devices: 216 us -> none  [per_device(): lax.psum_scatter(grad_w1, 'seq', scatter_dimension=0, tiled=True)]
    unnamed x4 -> x0, waiting for transfers between devices: 112 us -> none
    ppermute x33 -> x0, waiting for transfers between devices: 111 us -> none  [shifted(): lax.ppermute(x, axis, [(i, (i + by) % devices) for i in range(devices)])]
    psum x1 -> x0, waiting for transfers between devices: 88.8 us -> none  [per_device(): summed = lax.psum(partial_input, 'head')]
    ppermute x33 -> x0, starting transfers between devices: 83.8 us -> none  [shifted(): lax.ppermute(x, axis, [(i, (i + by) % devices) for i in range(devices)])]
    pallas_call x0 -> x1, Pallas kernels: none -> 82.3 us  [per_device(): pl.pallas_call(kernel, out_shape=(jax.ShapeDtypeStruct(tile, BF16), jax.S...]
    all_gather x1 -> x0, blocking collectives: 22.6 us -> none  [per_device(): full_grad = lax.all_gather(out_grad, 'head', axis=1, tiled=True)]
    reduce_or x16 -> x0, other arithmetic: 13.7 us -> none  [pair_terms(): return lax.cond(jnp.any(mask), work, skip, 0)]
  transfers between devices with their start and end apart: 36 -> 0, of which waited for: 35 -> 0; matrix products, arithmetic and copies ran while one was open for 4% -> 0% of each run, Pallas kernels for 0% -> 0%
where the time goes in v1:
time: 92 us; the launch traced here: 90.3 us
  Pallas kernels  82.3 us (89%)
  local copies, waits for them, and re-layouts  7.39 us (8%)
    pallas_call x1, Pallas kernels, per_device(): pl.pallas_call(kernel, out_shape=(jax.ShapeDtypeStruct(tile, BF16), jax.S...  82.3 us
    unnamed x15, local copies, waits for them, and re-layouts  7.39 us

profile of v1, /device:TPU:1, one launch (start us, length us, event | category | flops | bytes accessed | tf_op | source)
XLA Modules:
  0.0 90.3 jit_solution(8967002946813415571)
XLA Ops:
  0.6 0.0 copy-start
  0.6 1.2 %copy-done = bf16[1024,512]{1,0:T(8,128)(2,1)S(1)} copy-done((bf16[1024,512]{1,0:T(8,128)(2,1)S(1)}, bf16[1024,512]{1,0:T(8,128)(2,1)}, u32[]{:S(2)}) %copy-start) | copy-done | bytes 1048600
  1.9 0.0 copy-start.1
  1.9 1.0 %copy-done.1 = bf16[256,1024]{1,0:T(8,128)(2,1)S(1)} copy-done((bf16[256,1024]{1,0:T(8,128)(2,1)S(1)}, bf16[256,1024]{1,0:T(8,128)(2,1)}, u32[]{:S(2)}) %copy-start.1) | copy-done | bytes 524312
  2.9 0.0 copy-start.2
  2.9 0.9 %copy-done.2 = bf16[1024,128]{1,0:T(8,128)(2,1)S(1)} copy-done((bf16[1024,128]{1,0:T(8,128)(2,1)S(1)}, bf16[1024,128]{1,0:T(8,128)(2,1)}, u32[]{:S(2)}) %copy-start.2) | copy-done | bytes 262168
  3.9 0.0 copy-start.3
  3.9 0.8 copy-done.3
  4.7 0.0 copy-start.4
  4.7 0.8 copy-done.4
  5.5 0.0 copy-start.5
  5.5 0.7 copy-done.5
  6.2 82.3 %layer_backward.1 = (bf16[256,128]{1,0:T(8,128)(2,1)S(1)}, f32[16,512]{1,0:T(8,128)S(1)}, f32[16,128]{1,0:T(8,128)S(1)}) custom-call(bf16[256,1024]{1,0:T(8,128)(2,1)S(1)} %copy-done.1, bf16[256,128]{1,0:T(8,128)(2,1)S(1)} %copy-done.3, bf16[256,128]{1,0:T(8,128)(2,1)S(1)} %copy-done.4, bf16[1024,512]{1,0:T(8,128)(2,1)S(1)} %copy-done, ...), custom_call_target="tpu_custom_call" | custom-call | tf_op jit(solution)/shard_map/layer_backward/pallas_call | solution.py:429
  88.5 0.6 copy.12
  89.1 0.6 copy.13
  89.7 0.6 copy.14
Async XLA Ops:
  0.6 1.2 %copy-start = (bf16[1024,512]{1,0:T(8,128)(2,1)S(1)}, bf16[1024,512]{1,0:T(8,128)(2,1)}, u32[]{:S(2)}) copy-start(bf16[1024,512]{1,0:T(8,128)(2,1)} %wi.1) | copy-start | bytes 3145732
  1.9 1.0 %copy-start.1 = (bf16[256,1024]{1,0:T(8,128)(2,1)S(1)}, bf16[256,1024]{1,0:T(8,128)(2,1)}, u32[]{:S(2)}) copy-start(bf16[256,1024]{1,0:T(8,128)(2,1)} %ev.1) | copy-start | bytes 1572868
  2.9 0.9 %copy-start.2 = (bf16[1024,128]{1,0:T(8,128)(2,1)S(1)}, bf16[1024,128]{1,0:T(8,128)(2,1)}, u32[]{:S(2)}) copy-start(bf16[1024,128]{1,0:T(8,128)(2,1)} %wo.1) | copy-start | bytes 786436
  3.9 0.8 copy-start.3
  4.7 0.8 copy-start.4
  5.5 0.7 copy-start.5

commit v2 on v1

--- a/solution.py
+++ b/solution.py
@@ -48,13 +48,15 @@
 
 
 def kernel(
-    ev, og, sa, wi, wo, lens, gi, g1, g2,
+    ev_h, og_h, sa_h, wi_h, wo_h, lens_h, gi, g1, g2,
+    ev, sa, wi, wo, lens,
     n8, nb, ntr, rsd, slope, upart, ahat_s, arstd_s, dproj,
-    fg, qa, doa, kva, kvg, dqs, dqr,
+    fg, qa, doa, kva, ktr, wts, slp, kvg, dqs, dqr,
     kvs1, kvr1, kvs2, kvr2,
     ge, ge1, ga1, ge2, ga2, ge3,
     gl, gl1, gb1, gl2, gb2, gl3,
     ps, pr, own, st, sr,
+    in_s, near,
     fg_s, fg_r, q_s, q_r, do_s, do_r, kv_s, kv_r, dq_s, dq_r, kx_s, kx_r,
     e12_s, e12_r, e3_s, e3_r, l12_s, l12_r, l3_s, l3_r, p_s, p_r, t_s, t_r,
 ):
@@ -78,31 +80,54 @@
         pl.semaphore_signal(barrier, inc=1, device_id=at_head(i), device_id_type=MESH)
     for i in range(1, 4):
         pl.semaphore_signal(barrier, inc=1, device_id=in_plane(i), device_id_type=MESH)
-    for i in range(1, PLANES):
+    for i in (1, PLANES - 1):
         pl.semaphore_signal(barrier, inc=1, device_id=at_z(i), device_id_type=MESH)
 
+    def greet(level, distance):
+        for i in (distance, PLANES - distance):
+            pl.semaphore_signal(
+                near.at[level], inc=1, device_id=at_z(i), device_id_type=MESH
+            )
+
+    loads = [
+        pltpu.make_async_copy(src, dst, in_s.at[i])
+        for i, (src, dst) in enumerate(
+            ((og_h, fg.at[0]), (ev_h, ev), (wi_h, wi), (wo_h, wo), (sa_h, sa), (lens_h, lens))
+        )
+    ]
+    for copy in loads:
+        copy.start()
+
     def norm_rows(i, carry):
-        r = pl.multiple_of(i * 32, 32)
-        x = ev[pl.ds(r, 32), :].astype(F32)
+        r = pl.multiple_of(i * 64, 64)
+        x = ev[pl.ds(r, 64), :].astype(F32)
         cent = x - jnp.mean(x, axis=1, keepdims=True)
         rstd = lax.rsqrt(jnp.mean(cent * cent, axis=1, keepdims=True) + EPS)
         normed = cent * rstd
-        nb[pl.ds(r, 32), :] = normed.astype(BF16)
+        nb[pl.ds(r, 64), :] = normed.astype(BF16)
         for j in range(HEADS):
-            n8[j, pl.ds(r, 32), :] = normed[:, j * HD : (j + 1) * HD]
-        rsd[pl.ds(r, 32), :] = jnp.broadcast_to(rstd, (32, HD))
+            n8[j, pl.ds(r, 64), :] = normed[:, j * HD : (j + 1) * HD]
+        rsd[pl.ds(r, 64), :] = jnp.broadcast_to(rstd, (64, HD))
         return carry
 
-    lax.fori_loop(0, TOK // 32, norm_rows, 0)
-
-    pl.semaphore_wait(barrier, HEADS - 1 + 3 + PLANES - 1)
+    loads[1].wait()
+    lax.fori_loop(0, 2, norm_rows, 0)
+
+    loads[0].wait()
+    pl.semaphore_wait(barrier, HEADS - 1 + 3 + 2)
+    greet(0, 1)
     fg_copies = [
-        push(og, fg.at[i], fg_s.at[i], fg_r.at[i], at_head(i)) for i in range(1, HEADS)
-    ]
-    for copy in fg_copies:
-        copy.start()
-
-    for part in (2, 3, 1, 0):
+        push(fg.at[0], fg.at[i], fg_s.at[i], fg_r.at[i], at_head(i)) for i in range(1, HEADS)
+    ]
+    for i in (6, 2, 7, 5, 3, 1, 4):
+        fg_copies[i - 1].start()
+
+    lax.fori_loop(2, 4, norm_rows, 0)
+    pl.semaphore_wait(near.at[0], 2)
+    greet(1, 2)
+
+    loads[2].wait()
+    for part in (3, 1, 2, 0):
         proj = nn(nb[...], wi[:, part * HD : (part + 1) * HD])
         sig = 0.5 * jnp.tanh(0.5 * proj) + 0.5
         act = (proj * sig).astype(BF16)
@@ -115,17 +140,24 @@
             qa[0] = act
         else:
             kva[0, 0] = act
-
-    q_copies = [
-        push(qa.at[0], qa.at[d], q_s.at[d], q_r.at[d], at_z(PLANES - d))
-        for d in range(REACH, 0, -1)
-    ]
-    kv_copies = [
-        push(kva.at[0], kva.at[i], kv_s.at[i], kv_r.at[i], in_plane(i)) for i in (3, 2, 1)
-    ]
-    for copy in kv_copies + q_copies:
-        copy.start()
-
+        if part == 1:
+            kv_copies = [
+                push(kva.at[0], kva.at[i], kv_s.at[i], kv_r.at[i], in_plane(i))
+                for i in (3, 2, 1)
+            ]
+            for copy in kv_copies:
+                copy.start()
+        elif part == 2:
+            pl.semaphore_wait(near.at[1], 2)
+            greet(2, 4)
+            q_copies = [
+                push(qa.at[0], qa.at[d], q_s.at[d], q_r.at[d], at_z(PLANES - d))
+                for d in range(REACH, 0, -1)
+            ]
+            for copy in q_copies:
+                copy.start()
+
+    loads[4].wait()
     attn = sa[...].astype(F32)
     cent = attn - jnp.mean(attn, axis=1, keepdims=True)
     arstd = lax.rsqrt(jnp.mean(cent * cent, axis=1, keepdims=True) + EPS)
@@ -139,8 +171,9 @@
 
     lax.fori_loop(0, HEADS, turn_columns, 0)
 
-    dout = nn(og[...], wo[pl.ds(pl.multiple_of(h * HD, HD), HD), :])
-    for i in range(1, HEADS):
+    loads[3].wait()
+    dout = nn(fg[0], wo[pl.ds(pl.multiple_of(h * HD, HD), HD), :])
+    for i in (1, 7, 4, 2, 6, 3, 5):
         fg_copies[i - 1].wait_recv()
         row = pl.multiple_of(((h + HEADS - i) % HEADS) * HD, HD)
         dout += nn(fg[i], wo[pl.ds(row, HD), :])
@@ -164,14 +197,16 @@
     dproj[:, 0:HD] = (dout * ahat * slope[0]).astype(BF16)
     gated = (ahat * upart[...]).astype(BF16)
     ge[:, :, :, 0:HD] = (nn(ntr[...], dproj[:, 0:HD])).astype(BF16).reshape(32, 2, 16, HD)
-    for i in range(HEADS):
+
+    def head_rows(i, carry):
         block = pl.ds(((h + HEADS - i) % HEADS) * 4, 4)
-        rows = og[...] if i == 0 else fg[i]
-        ge[block, :, :, HD : 2 * HD] = tn(rows, gated).astype(BF16).reshape(4, 2, 16, HD)
+        ge[block, :, :, HD : 2 * HD] = tn(fg[i], gated).astype(BF16).reshape(4, 2, 16, HD)
+        return carry
+
+    lax.fori_loop(0, HEADS, head_rows, 0)
 
     def sum_parts(whole, into, over):
-        one = push(whole.at[:, 1 - c], into, over[0].at[0], over[1].at[0], in_plane(1))
-        return one
+        return push(whole.at[:, 1 - c], into, over[0].at[0], over[1].at[0], in_plane(1))
 
     def add_first(whole, came, kept):
         def step(i, carry):
@@ -207,62 +242,79 @@
     e_first = sum_parts(ge, ge1, (e12_s, e12_r))
     e_first.start()
 
+    loads[5].wait()
     ends = []
     run = 0
     for i in range(NSEQ):
         run = run + lens[i]
         ends.append(run)
     own_plane = (z + PLANES // 2) % PLANES
-
-    for copy in kv_copies:
-        copy.wait_recv()
-
-    def attend(turn, carry):
-        d = jnp.where(turn == 0, 0, REACH + 1 - turn)
-
-        @pl.when(turn > 0)
-        def _():
-            push(qa.at[0], qa.at[d], q_s.at[d], q_r.at[d], at_z(d)).wait_recv()
-            push(doa.at[0], doa.at[d], do_s.at[d], do_r.at[d], at_z(d)).wait_recv()
-
+    lane = lax.broadcasted_iota(jnp.int32, (1, TOK), 1)
+    down = lax.broadcasted_iota(jnp.int32, (TOK, TOK), 0)
+
+    def weigh(d):
         queries = qa[d]
-        upstream = doa[d]
-        lane = lax.broadcasted_iota(jnp.int32, (1, TOK), 1)
         qpos = ((own_plane + d) % PLANES) * 1024 + xh * 512 + c * 256 + lane
         first = jnp.zeros((1, TOK), jnp.int32)
         for end in ends:
             first = jnp.maximum(first, jnp.where(qpos >= end, end, 0))
 
-        def block(i, grad_q):
-            keys = kva[i, 0]
-            values = kva[i, 1]
-            kpos = (
-                own_plane * 1024
-                + ((xh + i // 2) % 2) * 512
-                + ((c + i) % 2) * 256
-                + lax.broadcasted_iota(jnp.int32, (TOK, TOK), 0)
-            )
-            mask = (kpos <= qpos) & (kpos >= first)
-            scores = nt(keys, queries) * SCALE
+        def block(i, carry):
+            base = own_plane * 1024 + ((xh + i // 2) % 2) * 512 + ((c + i) % 2) * 256
+            mask = (down <= qpos - base) & (down >= first - base)
+            scores = nt(kva[i, 0], queries) * SCALE
             sig = 0.5 * jnp.tanh(0.5 * scores) + 0.5
             weight = scores * sig
-            dprob = nt(values, upstream)
-            dscore = jnp.where(mask, dprob * (sig + weight * (1.0 - sig)), 0.0).astype(BF16)
-            weight = jnp.where(mask, weight, 0.0).astype(BF16)
+            slp[d, i] = jnp.where(mask, sig + weight * (1.0 - sig), 0.0)
+            wts[d, i] = jnp.where(mask, weight, 0.0).astype(BF16)
+            return carry
+
+        lax.fori_loop(0, 4, block, 0)
+
+    def gather_grads(d):
+        queries = qa[d]
+        upstream = doa[d]
+        grad_q = jnp.zeros((HD, TOK), F32)
+        for i in range(4):
+            dscore = (nt(kva[i, 1], upstream) * slp[d, i]).astype(BF16)
             kvg[i, 0] += nn(dscore, queries)
-            kvg[i, 1] += nn(weight, upstream)
-            return grad_q + tn(dscore, keys)
-
-        grad_q = lax.fori_loop(0, 4, block, jnp.zeros((TOK, HD), F32))
+            kvg[i, 1] += nn(wts[d, i], upstream)
+            grad_q += nn(ktr[i], dscore)
         dqs[d] = grad_q.astype(BF16)
 
-        @pl.when(turn > 0)
-        def _():
-            push(dqs.at[d], dqr.at[d], dq_s.at[d], dq_r.at[d], at_z(d)).start()
-
+    for copy in kv_copies:
+        copy.wait_recv()
+    for i in range(4):
+        ktr[i] = kva[i, 0].astype(F32).T.astype(BF16)
+    weigh(0)
+
+    e_first.wait_recv()
+    add_first(ge, ge1, ga1)
+    e_second = sum_across(ga1, ge2, (e12_s, e12_r))
+    e_second.start()
+
+    gather_grads(0)
+
+    def weigh_step(turn, carry):
+        d = REACH - turn
+        push(qa.at[0], qa.at[d], q_s.at[d], q_r.at[d], at_z(d)).wait_recv()
+        weigh(d)
         return carry
 
-    lax.fori_loop(0, REACH + 1, attend, 0)
+    lax.fori_loop(0, REACH, weigh_step, 0)
+
+    e_second.wait_recv()
+    add_second(ga1, ge2, ga2)
+    pl.semaphore_wait(near.at[2], 2)
+
+    def grads_step(turn, carry):
+        d = REACH - turn
+        push(doa.at[0], doa.at[d], do_s.at[d], do_r.at[d], at_z(d)).wait_recv()
+        gather_grads(d)
+        push(dqs.at[d], dqr.at[d], dq_s.at[d], dq_r.at[d], at_z(d)).start()
+        return carry
+
+    lax.fori_loop(0, REACH, grads_step, 0)
 
     for j in range(2):
         other = 2 * j + 1
@@ -270,10 +322,9 @@
     k_first = push(kvs1, kvr1, kx_s.at[0], kx_r.at[0], in_plane(1))
     k_first.start()
 
-    e_first.wait_recv()
-    add_first(ge, ge1, ga1)
-    e_second = sum_across(ga1, ge2, (e12_s, e12_r))
-    e_second.start()
+    e_third = sum_planes(ga2, ge3, (e3_s, e3_r))
+    for copy in e_third:
+        copy.start()
 
     k_first.wait_recv()
     kvs2[...] = (kvg[2] + kvr1[1].astype(F32)).astype(BF16)
@@ -287,16 +338,10 @@
     for d in range(REACH, 0, -1):
         dq_copies[d - 1].wait_recv()
         grad_q += dqr[d].astype(F32)
-    dproj[:, 2 * HD : 3 * HD] = (grad_q * (SCALE / MOST) * slope[2]).astype(BF16)
+    dproj[:, 2 * HD : 3 * HD] = (grad_q.T * (SCALE / MOST) * slope[2]).astype(BF16)
     gl[:, :, :, HD : 2 * HD] = (
         nn(ntr[...], dproj[:, 2 * HD : 3 * HD]).astype(BF16).reshape(32, 2, 16, HD)
     )
-
-    e_second.wait_recv()
-    add_second(ga1, ge2, ga2)
-    e_third = sum_planes(ga2, ge3, (e3_s, e3_r))
-    for copy in e_third:
-        copy.start()
 
     k_second.wait_recv()
     grad_k = kvg[0, 0] + kvr1[0, 0].astype(F32) + kvr2[0].astype(F32)
@@ -311,11 +356,10 @@
     total = jnp.zeros((TOK, HD), F32)
     along = jnp.zeros((TOK, HD), F32)
     p_copies = []
-    for i in (6, 2, 7, 5, 3, 1, 4, 0):
+
+    def spread(i, total, along):
         hh = (h + i) % HEADS
         part = nt(dproj[...], wi[pl.ds(pl.multiple_of(hh * HD, HD), HD), :])
-        total += part
-        along += part * n8[hh]
         if i:
             ps[i] = part.astype(BF16)
             copy = push(ps.at[i], pr.at[i], p_s.at[i], p_r.at[i], at_head(i))
@@ -323,6 +367,18 @@
             p_copies.append((i, copy))
         else:
             own[...] = part
+        return total + part, along + part * n8[hh]
+
+    for i in (6, 2, 7):
+        total, along = spread(i, total, along)
+
+    l_first.wait_recv()
+    add_first(gl, gl1, gb1)
+    l_second = sum_across(gb1, gl2, (l12_s, l12_r))
+    l_second.start()
+
+    for i in (5, 3, 1, 4, 0):
+        total, along = spread(i, total, along)
     lane = lax.broadcasted_iota(jnp.int32, (TOK, HD), 1)
     both = jnp.where(
         lane == 0,
@@ -335,11 +391,6 @@
     ]
     for copy in t_copies:
         copy.start()
-
-    l_first.wait_recv()
-    add_first(gl, gl1, gb1)
-    l_second = sum_across(gb1, gl2, (l12_s, l12_r))
-    l_second.start()
 
     for copy in e_third:
         copy.wait_recv()
@@ -363,20 +414,22 @@
         stats += sr[i]
     wide = jnp.concatenate([stats, jnp.zeros((HD - 8, TOK), F32)], axis=0).T * (1.0 / WIDTH)
     back = (summed - wide[:, 0:1] - n8[h] * wide[:, 1:2]) * rsd[...]
-    gi[...] = (og[...].astype(F32) + back).astype(BF16)
-
-    for copy in l_third:
-        copy.wait_recv()
-    late = add_third(gb2, gl3)
-    g1[:, HD:] = late
+    gi[...] = (fg[0].astype(F32) + back).astype(BF16)
 
     for copy in (
-        fg_copies + q_copies + kv_copies + do_copies + dq_copies + e_third + l_third + t_copies
+        fg_copies + q_copies + kv_copies + do_copies + dq_copies + e_third + t_copies
     ):
         copy.wait_send()
     for i, copy in p_copies:
         copy.wait_send()
     for copy in (e_first, e_second, k_first, k_second, l_first, l_second):
+        copy.wait_send()
+
+    for copy in l_third:
+        copy.wait_recv()
+    late = add_third(gb2, gl3)
+    g1[:, HD:] = late
+    for copy in l_third:
         copy.wait_send()
 
 
@@ -396,6 +449,11 @@
     vmem = pl.BlockSpec(memory_space=pltpu.VMEM)
     dma = pltpu.SemaphoreType.DMA
     scratch = [
+        pltpu.VMEM((TOK, WIDTH), BF16),
+        pltpu.VMEM(tile, BF16),
+        pltpu.VMEM((WIDTH, 4 * HD), BF16),
+        pltpu.VMEM((WIDTH, HD), BF16),
+        pltpu.SMEM((NSEQ,), jnp.int32),
         pltpu.VMEM((HEADS,) + tile, F32),
         pltpu.VMEM((TOK, WIDTH), BF16),
         pltpu.VMEM((WIDTH, TOK), BF16),
@@ -409,9 +467,12 @@
         pltpu.VMEM((REACH + 1,) + tile, BF16),
         pltpu.VMEM((REACH + 1,) + tile, BF16),
         pltpu.VMEM((4, 2) + tile, BF16),
+        pltpu.VMEM((4, HD, TOK), BF16),
+        pltpu.VMEM((REACH + 1, 4, TOK, TOK), BF16),
+        pltpu.VMEM((REACH + 1, 4, TOK, TOK), F32),
         pltpu.VMEM((4, 2) + tile, F32),
-        pltpu.VMEM((REACH + 1,) + tile, BF16),
-        pltpu.VMEM((REACH + 1,) + tile, BF16),
+        pltpu.VMEM((REACH + 1, HD, TOK), BF16),
+        pltpu.VMEM((REACH + 1, HD, TOK), BF16),
         pltpu.VMEM((2, 2) + tile, BF16),
         pltpu.VMEM((2, 2) + tile, BF16),
         pltpu.VMEM((2,) + tile, BF16),
@@ -425,6 +486,7 @@
         pltpu.VMEM((HEADS, 8, TOK), F32),
     ]
     counts = (8, 8, 5, 5, 5, 5, 4, 4, 5, 5, 2, 2, 2, 2, 16, 16, 2, 2, 16, 16, 8, 8, 8, 8)
+    scratch += [dma((6,)), pltpu.SemaphoreType.REGULAR((3,))]
     scratch += [dma((n,)) for n in counts]
     return pl.pallas_call(
         kernel,
@@ -433,11 +495,11 @@
             jax.ShapeDtypeStruct((16, 4 * HD), F32),
             jax.ShapeDtypeStruct((16, HD), F32),
         ),
-        in_specs=[vmem] * 5 + [pl.BlockSpec(memory_space=pltpu.SMEM)],
+        in_specs=[pl.BlockSpec(memory_space=pl.ANY)] * 6,
         out_specs=(vmem,) * 3,
         scratch_shapes=scratch,
         compiler_params=pltpu.CompilerParams(
-            collective_id=0, has_side_effects=True, vmem_limit_bytes=48 * 2**20
+            collective_id=0, has_side_effects=True, vmem_limit_bytes=56 * 2**20
         ),
         name="layer_backward",
     )(events, out_grad, saved_attn, in_weight, out_weight, lengths)

time: 92 us -> 85.6 us (0.930)
  local copies, waits for them, and re-layouts: 7.39 us -> 2.79 us
  Pallas kernels: 82.3 us -> 81.2 us
    unnamed x15 -> x7, local copies, waits for them, and re-layouts: 7.39 us -> 2.79 us
    pallas_call x1, Pallas kernels: 82.3 us -> 81.2 us  [per_device(): pl.pallas_call(kernel, out_shape=(jax.ShapeDtypeStruct(tile, BF16), jax.S...]
where the time goes in v2:
time: 85.6 us; the launch traced here: 84.6 us
  Pallas kernels  81.2 us (95%)
  local copies, waits for them, and re-layouts  2.79 us (3%)
    pallas_call x1, Pallas kernels, per_device(): pl.pallas_call(kernel, out_shape=(jax.ShapeDtypeStruct(tile, BF16), jax.S...  81.2 us
    unnamed x7, local copies, waits for them, and re-layouts  2.79 us

profile of v2, /device:TPU:1, one launch (start us, length us, event | category | flops | bytes accessed | tf_op | source)
XLA Modules:
  0.0 84.6 jit_solution(12520355441914612963)
XLA Ops:
  0.6 81.2 %layer_backward.1 = (bf16[256,128]{1,0:T(8,128)(2,1)}, f32[16,512]{1,0:T(8,128)}, f32[16,128]{1,0:T(8,128)}) custom-call(bf16[256,1024]{1,0:T(8,128)(2,1)} %ev_h.1, bf16[256,128]{1,0:T(8,128)(2,1)} %og_h.1, bf16[256,128]{1,0:T(8,128)(2,1)} %sa_h.1, bf16[1024,512]{1,0:T(8,128)(2,1)} %wi_h.1, bf16[1024,128]{1,0:T(8,128)(2,1)} %wo_h.1, s32[16]{0:T(128)} %lens_h.1), custom_call_target="tpu_custom_call" | custom-call | tf_op jit(solution)/shard_map/layer_backward/pallas_call | solution.py:491
  81.8 0.0 copy-start
  81.8 1.5 %copy.12 = bf16[256,128]{1,0:T(8,128)(2,1)} copy(bf16[256,128]{1,0:T(8,128)(2,1)} %get-tuple-element.6) | data formatting | bytes 131072
  83.3 0.0 copy-done
  83.3 0.0 copy-start.1
  83.3 0.6 copy.13
  83.9 0.1 copy-done.1
  84.0 0.6 copy.14
Async XLA Ops:
  81.8 1.5 %copy-start = (f32[16,512]{1,0:T(8,128)S(1)}, f32[16,512]{1,0:T(8,128)}, u32[]{:S(2)}) copy-start(f32[16,512]{1,0:T(8,128)} %get-tuple-element.7) | copy-start | bytes 98308
  83.3 0.7 copy-start.1

commit v3 on v2

--- a/solution.py
+++ b/solution.py
@@ -50,13 +50,13 @@
 def kernel(
     ev_h, og_h, sa_h, wi_h, wo_h, lens_h, gi, g1, g2,
     ev, sa, wi, wo, lens,
-    n8, nb, ntr, rsd, slope, upart, ahat_s, arstd_s, dproj,
+    n8, nb, ntr, rsd, slope, rates, rates_in, upart, ahat_s, arstd_s, dproj,
     fg, qa, doa, kva, ktr, wts, slp, kvg, dqs, dqr,
     kvs1, kvr1, kvs2, kvr2,
     ge, ge1, ga1, ge2, ga2, ge3,
     gl, gl1, gb1, gl2, gb2, gl3,
     ps, pr, own, st, sr,
-    in_s, near,
+    in_s, near, x_s, x_r,
     fg_s, fg_r, q_s, q_r, do_s, do_r, kv_s, kv_r, dq_s, dq_r, kx_s, kx_r,
     e12_s, e12_r, e3_s, e3_r, l12_s, l12_r, l3_s, l3_r, p_s, p_r, t_s, t_r,
 ):
@@ -126,12 +126,18 @@
     pl.semaphore_wait(near.at[0], 2)
     greet(1, 2)
 
+    def hop_queries(d):
+        return push(qa.at[d], qa.at[d + 1], q_s.at[d], q_r.at[d + 1], at_z(PLANES - 1))
+
     loads[2].wait()
     for part in (3, 1, 2, 0):
         proj = nn(nb[...], wi[:, part * HD : (part + 1) * HD])
         sig = 0.5 * jnp.tanh(0.5 * proj) + 0.5
         act = (proj * sig).astype(BF16)
-        slope[part] = sig * (1.0 + proj * (1.0 - sig))
+        rate = sig * (1.0 + proj * (1.0 - sig))
+        slope[part] = rate
+        if part in (1, 3):
+            rates[part // 2] = rate.astype(BF16)
         if part == 0:
             upart[...] = act.astype(F32)
         elif part == 1:
@@ -148,14 +154,7 @@
             for copy in kv_copies:
                 copy.start()
         elif part == 2:
-            pl.semaphore_wait(near.at[1], 2)
-            greet(2, 4)
-            q_copies = [
-                push(qa.at[0], qa.at[d], q_s.at[d], q_r.at[d], at_z(PLANES - d))
-                for d in range(REACH, 0, -1)
-            ]
-            for copy in q_copies:
-                copy.start()
+            hop_queries(0).start()
 
     loads[4].wait()
     attn = sa[...].astype(F32)
@@ -163,13 +162,8 @@
     arstd = lax.rsqrt(jnp.mean(cent * cent, axis=1, keepdims=True) + EPS)
     ahat_s[...] = cent * arstd
     arstd_s[...] = jnp.broadcast_to(arstd, (TOK, HD))
-    kvg[...] = jnp.zeros_like(kvg)
-
-    def turn_columns(j, carry):
-        ntr[pl.ds(pl.multiple_of(j * HD, HD), HD), :] = n8[j].T.astype(BF16)
-        return carry
-
-    lax.fori_loop(0, HEADS, turn_columns, 0)
+    pl.semaphore_wait(near.at[1], 2)
+    greet(2, 4)
 
     loads[3].wait()
     dout = nn(fg[0], wo[pl.ds(pl.multiple_of(h * HD, HD), HD), :])
@@ -193,10 +187,25 @@
     ]
     for copy in do_copies:
         copy.start()
+    hop_queries(0).wait_recv()
+    hop_queries(1).start()
+
+    def turn_columns(j, carry):
+        ntr[0, pl.ds(pl.multiple_of(j * HD, HD), HD), :] = n8[j].T.astype(BF16)
+        return carry
+
+    lax.fori_loop(0, HEADS, turn_columns, 0)
+    kvg[...] = jnp.zeros_like(kvg)
+    x_copies = [
+        push(ntr.at[0], ntr.at[1], x_s.at[0], x_r.at[0], in_plane(2)),
+        push(rates, rates_in, x_s.at[1], x_r.at[1], in_plane(2)),
+    ]
+    for copy in x_copies:
+        copy.start()
 
     dproj[:, 0:HD] = (dout * ahat * slope[0]).astype(BF16)
     gated = (ahat * upart[...]).astype(BF16)
-    ge[:, :, :, 0:HD] = (nn(ntr[...], dproj[:, 0:HD])).astype(BF16).reshape(32, 2, 16, HD)
+    ge[:, :, :, 0:HD] = (nn(ntr[0], dproj[:, 0:HD])).astype(BF16).reshape(32, 2, 16, HD)
 
     def head_rows(i, carry):
         block = pl.ds(((h + HEADS - i) % HEADS) * 4, 4)
@@ -287,6 +296,8 @@
     for i in range(4):
         ktr[i] = kva[i, 0].astype(F32).T.astype(BF16)
     weigh(0)
+    hop_queries(1).wait_recv()
+    hop_queries(2).start()
 
     e_first.wait_recv()
     add_first(ge, ge1, ga1)
@@ -296,8 +307,17 @@
     gather_grads(0)
 
     def weigh_step(turn, carry):
-        d = REACH - turn
-        push(qa.at[0], qa.at[d], q_s.at[d], q_r.at[d], at_z(d)).wait_recv()
+        d = turn + 1
+
+        @pl.when(d == REACH - 1)
+        def _():
+            hop_queries(2).wait_recv()
+            hop_queries(3).start()
+
+        @pl.when(d == REACH)
+        def _():
+            hop_queries(3).wait_recv()
+
         weigh(d)
         return carry
 
@@ -326,10 +346,29 @@
     for copy in e_third:
         copy.start()
 
+    for copy in x_copies:
+        copy.wait_recv()
     k_first.wait_recv()
-    kvs2[...] = (kvg[2] + kvr1[1].astype(F32)).astype(BF16)
+    mine = kvg[0] + kvr1[0].astype(F32)
+    other = kvg[2] + kvr1[1].astype(F32)
+    kvs2[...] = other.astype(BF16)
     k_second = push(kvs2, kvr2, kx_s.at[1], kx_r.at[1], in_plane(2))
     k_second.start()
+    key_scale = SCALE / MOST
+    value_scale = 1.0 / MOST
+    here = jnp.concatenate(
+        [mine[1] * value_scale * slope[1], mine[0] * key_scale * slope[3]], axis=1
+    ).astype(BF16)
+    there = jnp.concatenate(
+        [
+            other[1] * value_scale * rates_in[0].astype(F32),
+            other[0] * key_scale * rates_in[1].astype(F32),
+        ],
+        axis=1,
+    ).astype(BF16)
+    gl[:, :, :, 0 : 2 * HD] = (
+        (nn(ntr[0], here) + nn(ntr[1], there)).astype(BF16).reshape(32, 2, 16, 2 * HD)
+    )
 
     dq_copies = [
         push(dqs.at[d], dqr.at[d], dq_s.at[d], dq_r.at[d], at_z(d)) for d in range(1, REACH + 1)
@@ -338,20 +377,22 @@
     for d in range(REACH, 0, -1):
         dq_copies[d - 1].wait_recv()
         grad_q += dqr[d].astype(F32)
-    dproj[:, 2 * HD : 3 * HD] = (grad_q.T * (SCALE / MOST) * slope[2]).astype(BF16)
-    gl[:, :, :, HD : 2 * HD] = (
-        nn(ntr[...], dproj[:, 2 * HD : 3 * HD]).astype(BF16).reshape(32, 2, 16, HD)
+    dproj[:, 2 * HD : 3 * HD] = (grad_q.T * key_scale * slope[2]).astype(BF16)
+    gl[:, :, :, 2 * HD :] = (
+        nn(ntr[0], dproj[:, 2 * HD : 3 * HD]).astype(BF16).reshape(32, 2, 16, HD)
     )
-
-    k_second.wait_recv()
-    grad_k = kvg[0, 0] + kvr1[0, 0].astype(F32) + kvr2[0].astype(F32)
-    grad_v = kvg[0, 1] + kvr1[0, 1].astype(F32) + kvr2[1].astype(F32)
-    dproj[:, 3 * HD :] = (grad_k * (SCALE / MOST) * slope[3]).astype(BF16)
-    dproj[:, HD : 2 * HD] = (grad_v * (1.0 / MOST) * slope[1]).astype(BF16)
-    gl[:, :, :, 2 * HD :] = nn(ntr[...], dproj[:, 3 * HD :]).astype(BF16).reshape(32, 2, 16, HD)
-    gl[:, :, :, 0:HD] = nn(ntr[...], dproj[:, HD : 2 * HD]).astype(BF16).reshape(32, 2, 16, HD)
     l_first = sum_parts(gl, gl1, (l12_s, l12_r))
     l_first.start()
+    l_first.wait_recv()
+    add_first(gl, gl1, gb1)
+    l_second = sum_across(gb1, gl2, (l12_s, l12_r))
+    l_second.start()
+
+    k_second.wait_recv()
+    grad_k = mine[0] + kvr2[0].astype(F32)
+    grad_v = mine[1] + kvr2[1].astype(F32)
+    dproj[:, 3 * HD :] = (grad_k * key_scale * slope[3]).astype(BF16)
+    dproj[:, HD : 2 * HD] = (grad_v * value_scale * slope[1]).astype(BF16)
 
     total = jnp.zeros((TOK, HD), F32)
     along = jnp.zeros((TOK, HD), F32)
@@ -369,15 +410,7 @@
             own[...] = part
         return total + part, along + part * n8[hh]
 
-    for i in (6, 2, 7):
-        total, along = spread(i, total, along)
-
-    l_first.wait_recv()
-    add_first(gl, gl1, gb1)
-    l_second = sum_across(gb1, gl2, (l12_s, l12_r))
-    l_second.start()
-
-    for i in (5, 3, 1, 4, 0):
+    for i in (6, 2, 7, 5, 3, 1, 4, 0):
         total, along = spread(i, total, along)
     lane = lax.broadcasted_iota(jnp.int32, (TOK, HD), 1)
     both = jnp.where(
@@ -417,9 +450,11 @@
     gi[...] = (fg[0].astype(F32) + back).astype(BF16)
 
     for copy in (
-        fg_copies + q_copies + kv_copies + do_copies + dq_copies + e_third + t_copies
+        fg_copies + kv_copies + do_copies + dq_copies + e_third + t_copies + x_copies
     ):
         copy.wait_send()
+    for d in range(REACH):
+        hop_queries(d).wait_send()
     for i, copy in p_copies:
         copy.wait_send()
     for copy in (e_first, e_second, k_first, k_second, l_first, l_second):
@@ -428,7 +463,9 @@
     for copy in l_third:
         copy.wait_recv()
     late = add_third(gb2, gl3)
-    g1[:, HD:] = late
+    g1[:, HD : 2 * HD] = late[:, 0:HD]
+    g1[:, 2 * HD : 3 * HD] = late[:, 2 * HD :]
+    g1[:, 3 * HD :] = late[:, HD : 2 * HD]
     for copy in l_third:
         copy.wait_send()
 
@@ -456,9 +493,11 @@
         pltpu.SMEM((NSEQ,), jnp.int32),
         pltpu.VMEM((HEADS,) + tile, F32),
         pltpu.VMEM((TOK, WIDTH), BF16),
-        pltpu.VMEM((WIDTH, TOK), BF16),
+        pltpu.VMEM((2, WIDTH, TOK), BF16),
         pltpu.VMEM(tile, F32),
         pltpu.VMEM((4,) + tile, F32),
+        pltpu.VMEM((2,) + tile, BF16),
+        pltpu.VMEM((2,) + tile, BF16),
         pltpu.VMEM(tile, F32),
         pltpu.VMEM(tile, F32),
         pltpu.VMEM(tile, F32),
@@ -486,7 +525,7 @@
         pltpu.VMEM((HEADS, 8, TOK), F32),
     ]
     counts = (8, 8, 5, 5, 5, 5, 4, 4, 5, 5, 2, 2, 2, 2, 16, 16, 2, 2, 16, 16, 8, 8, 8, 8)
-    scratch += [dma((6,)), pltpu.SemaphoreType.REGULAR((3,))]
+    scratch += [dma((6,)), pltpu.SemaphoreType.REGULAR((3,)), dma((2,)), dma((2,))]
     scratch += [dma((n,)) for n in counts]
     return pl.pallas_call(
         kernel,

time: 85.6 us -> 91.2 us (1.065)
  Pallas kernels: 81.2 us -> 87.5 us
    pallas_call x1, Pallas kernels: 81.2 us -> 87.5 us  [per_device(): pl.pallas_call(kernel, out_shape=(jax.ShapeDtypeStruct(tile, BF16), jax.S...]
where the time goes in v3:
time: 91.2 us; the launch traced here: 91 us
  Pallas kernels  87.5 us (96%)
  local copies, waits for them, and re-layouts  2.79 us (3%)
    pallas_call x1, Pallas kernels, per_device(): pl.pallas_call(kernel, out_shape=(jax.ShapeDtypeStruct(tile, BF16), jax.S...  87.5 us
    unnamed x7, local copies, waits for them, and re-layouts  2.79 us

profile of v3, /device:TPU:1, one launch (start us, length us, event | category | flops | bytes accessed | tf_op | source)
XLA Modules:
  0.0 91.0 jit_solution(5887078235970843038)
XLA Ops:
  0.6 87.5 %layer_backward.1 = (bf16[256,128]{1,0:T(8,128)(2,1)}, f32[16,512]{1,0:T(8,128)}, f32[16,128]{1,0:T(8,128)}) custom-call(bf16[256,1024]{1,0:T(8,128)(2,1)} %ev_h.1, bf16[256,128]{1,0:T(8,128)(2,1)} %og_h.1, bf16[256,128]{1,0:T(8,128)(2,1)} %sa_h.1, bf16[1024,512]{1,0:T(8,128)(2,1)} %wi_h.1, bf16[1024,128]{1,0:T(8,128)(2,1)} %wo_h.1, s32[16]{0:T(128)} %lens_h.1), custom_call_target="tpu_custom_call" | custom-call | tf_op jit(solution)/shard_map/layer_backward/pallas_call | solution.py:530
  88.2 0.0 copy-start
  88.2 1.5 %copy.12 = bf16[256,128]{1,0:T(8,128)(2,1)} copy(bf16[256,128]{1,0:T(8,128)(2,1)} %get-tuple-element.6) | data formatting | bytes 131072
  89.6 0.0 copy-done
  89.6 0.0 copy-start.1
  89.7 0.6 copy.13
  90.3 0.1 copy-done.1
  90.4 0.6 copy.14
Async XLA Ops:
  88.2 1.5 %copy-start = (f32[16,512]{1,0:T(8,128)S(1)}, f32[16,512]{1,0:T(8,128)}, u32[]{:S(2)}) copy-start(f32[16,512]{1,0:T(8,128)} %get-tuple-element.7) | copy-start | bytes 98308
  89.6 0.7 copy-start.1

commit v4 on v2

--- a/solution.py
+++ b/solution.py
@@ -51,7 +51,7 @@
     ev_h, og_h, sa_h, wi_h, wo_h, lens_h, gi, g1, g2,
     ev, sa, wi, wo, lens,
     n8, nb, ntr, rsd, slope, upart, ahat_s, arstd_s, dproj,
-    fg, qa, doa, kva, ktr, wts, slp, kvg, dqs, dqr,
+    fg, qa, doa, kva, ktr, begin, rowpos, kvg, dqs, dqr,
     kvs1, kvr1, kvs2, kvr2,
     ge, ge1, ga1, ge2, ga2, ge3,
     gl, gl1, gb1, gl2, gb2, gl3,
@@ -125,6 +125,9 @@
     lax.fori_loop(2, 4, norm_rows, 0)
     pl.semaphore_wait(near.at[0], 2)
     greet(1, 2)
+
+    def hop_queries(d):
+        return push(qa.at[d], qa.at[d + 1], q_s.at[d], q_r.at[d + 1], at_z(PLANES - 1))
 
     loads[2].wait()
     for part in (3, 1, 2, 0):
@@ -148,14 +151,7 @@
             for copy in kv_copies:
                 copy.start()
         elif part == 2:
-            pl.semaphore_wait(near.at[1], 2)
-            greet(2, 4)
-            q_copies = [
-                push(qa.at[0], qa.at[d], q_s.at[d], q_r.at[d], at_z(PLANES - d))
-                for d in range(REACH, 0, -1)
-            ]
-            for copy in q_copies:
-                copy.start()
+            hop_queries(0).start()
 
     loads[4].wait()
     attn = sa[...].astype(F32)
@@ -163,13 +159,8 @@
     arstd = lax.rsqrt(jnp.mean(cent * cent, axis=1, keepdims=True) + EPS)
     ahat_s[...] = cent * arstd
     arstd_s[...] = jnp.broadcast_to(arstd, (TOK, HD))
-    kvg[...] = jnp.zeros_like(kvg)
-
-    def turn_columns(j, carry):
-        ntr[pl.ds(pl.multiple_of(j * HD, HD), HD), :] = n8[j].T.astype(BF16)
-        return carry
-
-    lax.fori_loop(0, HEADS, turn_columns, 0)
+    pl.semaphore_wait(near.at[1], 2)
+    greet(2, 4)
 
     loads[3].wait()
     dout = nn(fg[0], wo[pl.ds(pl.multiple_of(h * HD, HD), HD), :])
@@ -189,10 +180,18 @@
     ).astype(BF16)
     do_copies = [
         push(doa.at[0], doa.at[d], do_s.at[d], do_r.at[d], at_z(PLANES - d))
-        for d in range(REACH, 0, -1)
+        for d in (2, 4, 3, 1)
     ]
     for copy in do_copies:
         copy.start()
+    hop_queries(0).wait_recv()
+    hop_queries(1).start()
+
+    def turn_columns(j, carry):
+        ntr[pl.ds(pl.multiple_of(j * HD, HD), HD), :] = n8[j].T.astype(BF16)
+        return carry
+
+    lax.fori_loop(0, HEADS, turn_columns, 0)
 
     dproj[:, 0:HD] = (dout * ahat * slope[0]).astype(BF16)
     gated = (ahat * upart[...]).astype(BF16)
@@ -241,6 +240,9 @@
 
     e_first = sum_parts(ge, ge1, (e12_s, e12_r))
     e_first.start()
+
+    hop_queries(1).wait_recv()
+    hop_queries(2).start()
 
     loads[5].wait()
     ends = []
@@ -249,72 +251,83 @@
         run = run + lens[i]
         ends.append(run)
     own_plane = (z + PLANES // 2) % PLANES
-    lane = lax.broadcasted_iota(jnp.int32, (1, TOK), 1)
-    down = lax.broadcasted_iota(jnp.int32, (TOK, TOK), 0)
-
-    def weigh(d):
-        queries = qa[d]
-        qpos = ((own_plane + d) % PLANES) * 1024 + xh * 512 + c * 256 + lane
-        first = jnp.zeros((1, TOK), jnp.int32)
+
+    def history_starts(d, carry):
+        plane = own_plane + d
+        qpos = plane * 1024 + xh * 512 + c * 256 + lax.broadcasted_iota(jnp.int32, (8, TOK), 1)
+        first = jnp.zeros((8, TOK), jnp.int32)
         for end in ends:
             first = jnp.maximum(first, jnp.where(qpos >= end, end, 0))
-
-        def block(i, carry):
-            base = own_plane * 1024 + ((xh + i // 2) % 2) * 512 + ((c + i) % 2) * 256
-            mask = (down <= qpos - base) & (down >= first - base)
-            scores = nt(kva[i, 0], queries) * SCALE
-            sig = 0.5 * jnp.tanh(0.5 * scores) + 0.5
-            weight = scores * sig
-            slp[d, i] = jnp.where(mask, sig + weight * (1.0 - sig), 0.0)
-            wts[d, i] = jnp.where(mask, weight, 0.0).astype(BF16)
-            return carry
-
-        lax.fori_loop(0, 4, block, 0)
-
-    def gather_grads(d):
-        queries = qa[d]
-        upstream = doa[d]
-        grad_q = jnp.zeros((HD, TOK), F32)
-        for i in range(4):
-            dscore = (nt(kva[i, 1], upstream) * slp[d, i]).astype(BF16)
-            kvg[i, 0] += nn(dscore, queries)
-            kvg[i, 1] += nn(wts[d, i], upstream)
-            grad_q += nn(ktr[i], dscore)
-        dqs[d] = grad_q.astype(BF16)
+        begin[d] = jnp.where(plane < PLANES, first - own_plane * 1024, 2 * 1024)
+        return carry
+
+    lax.fori_loop(0, REACH + 1, history_starts, 0)
 
     for copy in kv_copies:
         copy.wait_recv()
     for i in range(4):
-        ktr[i] = kva[i, 0].astype(F32).T.astype(BF16)
-    weigh(0)
+        ktr[:, i * TOK : (i + 1) * TOK] = kva[i, 0].astype(F32).T.astype(BF16)
+
+    def slot_rows(shape):
+        row = lax.broadcasted_iota(jnp.int32, shape, 0)
+        half = row // 512
+        quarter = (row // 256) % 2
+        place = jnp.where(xh == 0, half, 1 - half) * 512
+        place += jnp.where(c == 0, quarter, 1 - quarter) * 256
+        return place + row % 256
+
+    rowpos[...] = slot_rows((4 * TOK, HD))
+
+    def attend(d, same):
+        queries = qa[d]
+        upstream = doa[d]
+        keys = kva[:, 0].reshape(4 * TOK, HD)
+        values = kva[:, 1].reshape(4 * TOK, HD)
+        down = jnp.concatenate([rowpos[...]] * 2, axis=1)
+        mask = down >= begin[d, 0:1, :]
+        if same:
+            lane = lax.broadcasted_iota(jnp.int32, (1, TOK), 1)
+            mask = mask & (down <= xh * 512 + c * 256 + lane)
+        half = nt(keys, queries) * (0.5 * SCALE)
+        bell = 1.0 + jnp.tanh(half)
+        weight = half * bell
+        sig = 0.5 * bell
+        dprob = nt(values, upstream)
+        dscore = jnp.where(mask, dprob * (sig + weight * (1.0 - sig)), 0.0).astype(BF16)
+        weight = jnp.where(mask, weight, 0.0).astype(BF16)
+        grad_k = nn(dscore, queries).reshape(4, TOK, HD)
+        grad_v = nn(weight, upstream).reshape(4, TOK, HD)
+        if same:
+            kvg[:, 0] = grad_k
+            kvg[:, 1] = grad_v
+        else:
+            kvg[:, 0] += grad_k
+            kvg[:, 1] += grad_v
+        dqs[d] = nn(ktr[...], dscore).astype(BF16)
+
+    attend(0, True)
 
     e_first.wait_recv()
     add_first(ge, ge1, ga1)
     e_second = sum_across(ga1, ge2, (e12_s, e12_r))
     e_second.start()
 
-    gather_grads(0)
-
-    def weigh_step(turn, carry):
-        d = REACH - turn
-        push(qa.at[0], qa.at[d], q_s.at[d], q_r.at[d], at_z(d)).wait_recv()
-        weigh(d)
-        return carry
-
-    lax.fori_loop(0, REACH, weigh_step, 0)
-
-    e_second.wait_recv()
-    add_second(ga1, ge2, ga2)
-    pl.semaphore_wait(near.at[2], 2)
-
-    def grads_step(turn, carry):
-        d = REACH - turn
+    hop_queries(2).wait_recv()
+    hop_queries(3).start()
+
+    def attend_step(turn, carry):
+        d = jnp.where(turn == 0, 2, jnp.where(turn == 1, 1, turn + 1))
+
+        @pl.when(d == REACH)
+        def _():
+            hop_queries(3).wait_recv()
+
         push(doa.at[0], doa.at[d], do_s.at[d], do_r.at[d], at_z(d)).wait_recv()
-        gather_grads(d)
+        attend(d, False)
         push(dqs.at[d], dqr.at[d], dq_s.at[d], dq_r.at[d], at_z(d)).start()
         return carry
 
-    lax.fori_loop(0, REACH, grads_step, 0)
+    lax.fori_loop(0, REACH, attend_step, 0)
 
     for j in range(2):
         other = 2 * j + 1
@@ -322,6 +335,9 @@
     k_first = push(kvs1, kvr1, kx_s.at[0], kx_r.at[0], in_plane(1))
     k_first.start()
 
+    e_second.wait_recv()
+    add_second(ga1, ge2, ga2)
+    pl.semaphore_wait(near.at[2], 2)
     e_third = sum_planes(ga2, ge3, (e3_s, e3_r))
     for copy in e_third:
         copy.start()
@@ -339,7 +355,7 @@
         dq_copies[d - 1].wait_recv()
         grad_q += dqr[d].astype(F32)
     dproj[:, 2 * HD : 3 * HD] = (grad_q.T * (SCALE / MOST) * slope[2]).astype(BF16)
-    gl[:, :, :, HD : 2 * HD] = (
+    gl[:, :, :, 2 * HD :] = (
         nn(ntr[...], dproj[:, 2 * HD : 3 * HD]).astype(BF16).reshape(32, 2, 16, HD)
     )
 
@@ -348,10 +364,14 @@
     grad_v = kvg[0, 1] + kvr1[0, 1].astype(F32) + kvr2[1].astype(F32)
     dproj[:, 3 * HD :] = (grad_k * (SCALE / MOST) * slope[3]).astype(BF16)
     dproj[:, HD : 2 * HD] = (grad_v * (1.0 / MOST) * slope[1]).astype(BF16)
-    gl[:, :, :, 2 * HD :] = nn(ntr[...], dproj[:, 3 * HD :]).astype(BF16).reshape(32, 2, 16, HD)
-    gl[:, :, :, 0:HD] = nn(ntr[...], dproj[:, HD : 2 * HD]).astype(BF16).reshape(32, 2, 16, HD)
+    pair = jnp.concatenate([dproj[:, HD : 2 * HD], dproj[:, 3 * HD :]], axis=1)
+    gl[:, :, :, 0 : 2 * HD] = nn(ntr[...], pair).astype(BF16).reshape(32, 2, 16, 2 * HD)
     l_first = sum_parts(gl, gl1, (l12_s, l12_r))
     l_first.start()
+    l_first.wait_recv()
+    add_first(gl, gl1, gb1)
+    l_second = sum_across(gb1, gl2, (l12_s, l12_r))
+    l_second.start()
 
     total = jnp.zeros((TOK, HD), F32)
     along = jnp.zeros((TOK, HD), F32)
@@ -369,15 +389,7 @@
             own[...] = part
         return total + part, along + part * n8[hh]
 
-    for i in (6, 2, 7):
-        total, along = spread(i, total, along)
-
-    l_first.wait_recv()
-    add_first(gl, gl1, gb1)
-    l_second = sum_across(gb1, gl2, (l12_s, l12_r))
-    l_second.start()
-
-    for i in (5, 3, 1, 4, 0):
+    for i in (6, 2, 7, 5, 3, 1, 4, 0):
         total, along = spread(i, total, along)
     lane = lax.broadcasted_iota(jnp.int32, (TOK, HD), 1)
     both = jnp.where(
@@ -417,9 +429,11 @@
     gi[...] = (fg[0].astype(F32) + back).astype(BF16)
 
     for copy in (
-        fg_copies + q_copies + kv_copies + do_copies + dq_copies + e_third + t_copies
+        fg_copies + kv_copies + do_copies + dq_copies + e_third + t_copies
     ):
         copy.wait_send()
+    for d in range(REACH):
+        hop_queries(d).wait_send()
     for i, copy in p_copies:
         copy.wait_send()
     for copy in (e_first, e_second, k_first, k_second, l_first, l_second):
@@ -428,7 +442,9 @@
     for copy in l_third:
         copy.wait_recv()
     late = add_third(gb2, gl3)
-    g1[:, HD:] = late
+    g1[:, HD : 2 * HD] = late[:, 0:HD]
+    g1[:, 2 * HD : 3 * HD] = late[:, 2 * HD :]
+    g1[:, 3 * HD :] = late[:, HD : 2 * HD]
     for copy in l_third:
         copy.wait_send()
 
@@ -467,9 +483,9 @@
         pltpu.VMEM((REACH + 1,) + tile, BF16),
         pltpu.VMEM((REACH + 1,) + tile, BF16),
         pltpu.VMEM((4, 2) + tile, BF16),
-        pltpu.VMEM((4, HD, TOK), BF16),
-        pltpu.VMEM((REACH + 1, 4, TOK, TOK), BF16),
-        pltpu.VMEM((REACH + 1, 4, TOK, TOK), F32),
+        pltpu.VMEM((HD, 4 * TOK), BF16),
+        pltpu.VMEM((REACH + 1, 8, TOK), jnp.int32),
+        pltpu.VMEM((4 * TOK, HD), jnp.int32),
         pltpu.VMEM((4, 2) + tile, F32),
         pltpu.VMEM((REACH + 1, HD, TOK), BF16),
         pltpu.VMEM((REACH + 1, HD, TOK), BF16),

time: 85.6 us -> 88 us (1.028)
  Pallas kernels: 81.2 us -> 84.3 us
    pallas_call x1, Pallas kernels: 81.2 us -> 84.3 us  [per_device(): pl.pallas_call(kernel, out_shape=(jax.ShapeDtypeStruct(tile, BF16), jax.S...]
where the time goes in v4:
time: 88 us; the launch traced here: 87.7 us
  Pallas kernels  84.3 us (96%)
  local copies, waits for them, and re-layouts  2.79 us (3%)
    pallas_call x1, Pallas kernels, per_device(): pl.pallas_call(kernel, out_shape=(jax.ShapeDtypeStruct(tile, BF16), jax.S...  84.3 us
    unnamed x7, local copies, waits for them, and re-layouts  2.79 us

profile of v4, /device:TPU:1, one launch (start us, length us, event | category | flops | bytes accessed | tf_op | source)
XLA Modules:
  0.0 87.7 jit_solution(18434506788117960179)
XLA Ops:
  0.6 84.3 %layer_backward.1 = (bf16[256,128]{1,0:T(8,128)(2,1)}, f32[16,512]{1,0:T(8,128)}, f32[16,128]{1,0:T(8,128)}) custom-call(bf16[256,1024]{1,0:T(8,128)(2,1)} %ev_h.1, bf16[256,128]{1,0:T(8,128)(2,1)} %og_h.1, bf16[256,128]{1,0:T(8,128)(2,1)} %sa_h.1, bf16[1024,512]{1,0:T(8,128)(2,1)} %wi_h.1, bf16[1024,128]{1,0:T(8,128)(2,1)} %wo_h.1, s32[16]{0:T(128)} %lens_h.1), custom_call_target="tpu_custom_call" | custom-call | tf_op jit(solution)/shard_map/layer_backward/pallas_call | solution.py:507
  84.9 0.0 copy-start
  85.0 1.5 %copy.12 = bf16[256,128]{1,0:T(8,128)(2,1)} copy(bf16[256,128]{1,0:T(8,128)(2,1)} %get-tuple-element.6) | data formatting | bytes 131072
  86.4 0.0 copy-done
  86.4 0.0 copy-start.1
  86.4 0.6 copy.13
  87.1 0.1 copy-done.1
  87.2 0.6 copy.14
Async XLA Ops:
  84.9 1.5 %copy-start = (f32[16,512]{1,0:T(8,128)S(1)}, f32[16,512]{1,0:T(8,128)}, u32[]{:S(2)}) copy-start(f32[16,512]{1,0:T(8,128)} %get-tuple-element.7) | copy-start | bytes 98308
  86.4 0.7 copy-start.1

commit v5 on v4

--- a/solution.py
+++ b/solution.py
@@ -126,8 +126,10 @@
     pl.semaphore_wait(near.at[0], 2)
     greet(1, 2)
 
-    def hop_queries(d):
-        return push(qa.at[d], qa.at[d + 1], q_s.at[d], q_r.at[d + 1], at_z(PLANES - 1))
+    def hop_queries(d, by):
+        return push(
+            qa.at[d], qa.at[d + by], q_s.at[d + by], q_r.at[d + by], at_z(PLANES - by)
+        )
 
     loads[2].wait()
     for part in (3, 1, 2, 0):
@@ -151,7 +153,8 @@
             for copy in kv_copies:
                 copy.start()
         elif part == 2:
-            hop_queries(0).start()
+            hop_queries(0, 2).start()
+            hop_queries(0, 1).start()
 
     loads[4].wait()
     attn = sa[...].astype(F32)
@@ -178,14 +181,17 @@
         )
         * arstd_s[...]
     ).astype(BF16)
-    do_copies = [
-        push(doa.at[0], doa.at[d], do_s.at[d], do_r.at[d], at_z(PLANES - d))
-        for d in (2, 4, 3, 1)
-    ]
-    for copy in do_copies:
-        copy.start()
-    hop_queries(0).wait_recv()
-    hop_queries(1).start()
+    def hop_upstream(d, by):
+        return push(
+            doa.at[d], doa.at[d + by], do_s.at[d + by], do_r.at[d + by], at_z(PLANES - by)
+        )
+
+    hop_upstream(0, 2).start()
+    hop_upstream(0, 1).start()
+    hop_queries(0, 2).wait_recv()
+    hop_queries(2, 2).start()
+    hop_queries(0, 1).wait_recv()
+    hop_queries(1, 2).start()
 
     def turn_columns(j, carry):
         ntr[pl.ds(pl.multiple_of(j * HD, HD), HD), :] = n8[j].T.astype(BF16)
@@ -240,9 +246,6 @@
 
     e_first = sum_parts(ge, ge1, (e12_s, e12_r))
     e_first.start()
-
-    hop_queries(1).wait_recv()
-    hop_queries(2).start()
 
     loads[5].wait()
     ends = []
@@ -305,6 +308,10 @@
             kvg[:, 1] += grad_v
         dqs[d] = nn(ktr[...], dscore).astype(BF16)
 
+    hop_upstream(0, 2).wait_recv()
+    hop_upstream(2, 2).start()
+    hop_upstream(0, 1).wait_recv()
+    hop_upstream(1, 2).start()
     attend(0, True)
 
     e_first.wait_recv()
@@ -312,17 +319,19 @@
     e_second = sum_across(ga1, ge2, (e12_s, e12_r))
     e_second.start()
 
-    hop_queries(2).wait_recv()
-    hop_queries(3).start()
-
     def attend_step(turn, carry):
-        d = jnp.where(turn == 0, 2, jnp.where(turn == 1, 1, turn + 1))
-
-        @pl.when(d == REACH)
+        d = jnp.where(turn < 2, 2 - turn, 6 - turn)
+
+        @pl.when(d == 4)
         def _():
-            hop_queries(3).wait_recv()
-
-        push(doa.at[0], doa.at[d], do_s.at[d], do_r.at[d], at_z(d)).wait_recv()
+            hop_queries(2, 2).wait_recv()
+            hop_upstream(2, 2).wait_recv()
+
+        @pl.when(d == 3)
+        def _():
+            hop_queries(1, 2).wait_recv()
+            hop_upstream(1, 2).wait_recv()
+
         attend(d, False)
         push(dqs.at[d], dqr.at[d], dq_s.at[d], dq_r.at[d], at_z(d)).start()
         return carry
@@ -335,12 +344,6 @@
     k_first = push(kvs1, kvr1, kx_s.at[0], kx_r.at[0], in_plane(1))
     k_first.start()
 
-    e_second.wait_recv()
-    add_second(ga1, ge2, ga2)
-    pl.semaphore_wait(near.at[2], 2)
-    e_third = sum_planes(ga2, ge3, (e3_s, e3_r))
-    for copy in e_third:
-        copy.start()
 
     k_first.wait_recv()
     kvs2[...] = (kvg[2] + kvr1[1].astype(F32)).astype(BF16)
@@ -372,6 +375,12 @@
     add_first(gl, gl1, gb1)
     l_second = sum_across(gb1, gl2, (l12_s, l12_r))
     l_second.start()
+    e_second.wait_recv()
+    add_second(ga1, ge2, ga2)
+    pl.semaphore_wait(near.at[2], 2)
+    e_third = sum_planes(ga2, ge3, (e3_s, e3_r))
+    for copy in e_third:
+        copy.start()
 
     total = jnp.zeros((TOK, HD), F32)
     along = jnp.zeros((TOK, HD), F32)
@@ -429,11 +438,12 @@
     gi[...] = (fg[0].astype(F32) + back).astype(BF16)
 
     for copy in (
-        fg_copies + kv_copies + do_copies + dq_copies + e_third + t_copies
+        fg_copies + kv_copies + dq_copies + e_third + t_copies
     ):
         copy.wait_send()
-    for d in range(REACH):
-        hop_queries(d).wait_send()
+    for d, by in ((0, 1), (0, 2), (1, 2), (2, 2)):
+        hop_queries(d, by).wait_send()
+        hop_upstream(d, by).wait_send()
     for i, copy in p_copies:
         copy.wait_send()
     for copy in (e_first, e_second, k_first, k_second, l_first, l_second):

time: 88 us -> 78.7 us (0.89)
  Pallas kernels: 84.3 us -> 75 us
    pallas_call x1, Pallas kernels: 84.3 us -> 75 us  [per_device(): pl.pallas_call(kernel, out_shape=(jax.ShapeDtypeStruct(tile, BF16), jax.S...]
where the time goes in v5:
time: 78.7 us; the launch traced here: 78.5 us
  Pallas kernels  75 us (95%)
  local copies, waits for them, and re-layouts  2.79 us (4%)
    pallas_call x1, Pallas kernels, per_device(): pl.pallas_call(kernel, out_shape=(jax.ShapeDtypeStruct(tile, BF16), jax.S...  75 us
    unnamed x7, local copies, waits for them, and re-layouts  2.79 us

profile of v5, /device:TPU:1, one launch (start us, length us, event | category | flops | bytes accessed | tf_op | source)
XLA Modules:
  0.0 78.5 jit_solution(1903654205707788763)
XLA Ops:
  0.6 75.0 %layer_backward.1 = (bf16[256,128]{1,0:T(8,128)(2,1)}, f32[16,512]{1,0:T(8,128)}, f32[16,128]{1,0:T(8,128)}) custom-call(bf16[256,1024]{1,0:T(8,128)(2,1)} %ev_h.1, bf16[256,128]{1,0:T(8,128)(2,1)} %og_h.1, bf16[256,128]{1,0:T(8,128)(2,1)} %sa_h.1, bf16[1024,512]{1,0:T(8,128)(2,1)} %wi_h.1, bf16[1024,128]{1,0:T(8,128)(2,1)} %wo_h.1, s32[16]{0:T(128)} %lens_h.1), custom_call_target="tpu_custom_call" | custom-call | tf_op jit(solution)/shard_map/layer_backward/pallas_call | solution.py:517
  75.7 0.0 copy-start
  75.7 1.5 %copy.12 = bf16[256,128]{1,0:T(8,128)(2,1)} copy(bf16[256,128]{1,0:T(8,128)(2,1)} %get-tuple-element.6) | data formatting | bytes 131072
  77.2 0.0 copy-done
  77.2 0.0 copy-start.1
  77.2 0.6 copy.13
  77.8 0.1 copy-done.1
  77.9 0.6 copy.14
Async XLA Ops:
  75.7 1.5 %copy-start = (f32[16,512]{1,0:T(8,128)S(1)}, f32[16,512]{1,0:T(8,128)}, u32[]{:S(2)}) copy-start(f32[16,512]{1,0:T(8,128)} %get-tuple-element.7) | copy-start | bytes 98308
  77.2 0.7 copy-start.1

commit v6 on v5

--- a/solution.py
+++ b/solution.py
@@ -22,6 +22,8 @@
 F32 = jnp.float32
 BF16 = jnp.bfloat16
 NEAR_LAST = (8, 7, 9, 6, 10, 5, 11, 4, 12, 3, 13, 2, 14, 1, 15)
+FAR = 4
+FAR_COUNT = 9
 
 
 def nn(a, b):
@@ -214,32 +216,42 @@
         return push(whole.at[:, 1 - c], into, over[0].at[0], over[1].at[0], in_plane(1))
 
     def add_first(whole, came, kept):
-        def step(i, carry):
-            kept[i] = (
-                whole[pl.ds(2 * i, 2), c].astype(F32) + came[pl.ds(2 * i, 2)].astype(F32)
-            ).astype(BF16)
+        def step(k, carry):
+            rows = pl.ds(2 * ((z + k + FAR) % PLANES), 2)
+            kept[k] = (whole[rows, c].astype(F32) + came[rows].astype(F32)).astype(BF16)
             return carry
 
         lax.fori_loop(0, PLANES, step, 0)
 
     def sum_across(kept, into, over):
-        return push(kept.at[:, 1 - xh], into, over[0].at[1], over[1].at[1], in_plane(2))
-
-    def add_second(kept, came, final):
-        def step(i, carry):
-            final[i] = (kept[i, xh].astype(F32) + came[i].astype(F32)).astype(BF16)
+        return [
+            push(
+                kept.at[pl.ds(low, count), 1 - xh],
+                into.at[pl.ds(low, count)],
+                over[0].at[i],
+                over[1].at[i],
+                in_plane(2),
+            )
+            for i, low, count in ((1, 0, FAR_COUNT), (2, FAR_COUNT, PLANES - FAR_COUNT))
+        ]
+
+    def add_second(kept, came, final, low, high):
+        def step(k, carry):
+            final[k] = (kept[k, xh].astype(F32) + came[k].astype(F32)).astype(BF16)
             return carry
 
-        lax.fori_loop(0, PLANES, step, 0)
+        lax.fori_loop(low, high, step, 0)
 
     def sum_planes(final, into, over):
         return [
-            push(final.at[(z + i) % PLANES], into.at[i], over[0].at[i], over[1].at[i], at_z(i))
+            push(
+                final.at[(i - FAR) % PLANES], into.at[i], over[0].at[i], over[1].at[i], at_z(i)
+            )
             for i in NEAR_LAST
         ]
 
     def add_third(final, came):
-        total = final[z].astype(F32)
+        total = final[PLANES - FAR].astype(F32)
         for i in range(1, PLANES):
             total += came[i].astype(F32)
         return total * GRAD_SCALE
@@ -317,7 +329,8 @@
     e_first.wait_recv()
     add_first(ge, ge1, ga1)
     e_second = sum_across(ga1, ge2, (e12_s, e12_r))
-    e_second.start()
+    for copy in e_second:
+        copy.start()
 
     def attend_step(turn, carry):
         d = jnp.where(turn < 2, 2 - turn, 6 - turn)
@@ -350,6 +363,11 @@
     k_second = push(kvs2, kvr2, kx_s.at[1], kx_r.at[1], in_plane(2))
     k_second.start()
 
+    for copy in e_second:
+        copy.wait_recv()
+    add_second(ga1, ge2, ga2, 0, PLANES)
+    pl.semaphore_wait(near.at[2], 2)
+    e_third = sum_planes(ga2, ge3, (e3_s, e3_r))
     dq_copies = [
         push(dqs.at[d], dqr.at[d], dq_s.at[d], dq_r.at[d], at_z(d)) for d in range(1, REACH + 1)
     ]
@@ -357,6 +375,8 @@
     for d in range(REACH, 0, -1):
         dq_copies[d - 1].wait_recv()
         grad_q += dqr[d].astype(F32)
+    for copy in e_third:
+        copy.start()
     dproj[:, 2 * HD : 3 * HD] = (grad_q.T * (SCALE / MOST) * slope[2]).astype(BF16)
     gl[:, :, :, 2 * HD :] = (
         nn(ntr[...], dproj[:, 2 * HD : 3 * HD]).astype(BF16).reshape(32, 2, 16, HD)
@@ -374,12 +394,7 @@
     l_first.wait_recv()
     add_first(gl, gl1, gb1)
     l_second = sum_across(gb1, gl2, (l12_s, l12_r))
-    l_second.start()
-    e_second.wait_recv()
-    add_second(ga1, ge2, ga2)
-    pl.semaphore_wait(near.at[2], 2)
-    e_third = sum_planes(ga2, ge3, (e3_s, e3_r))
-    for copy in e_third:
+    for copy in l_second:
         copy.start()
 
     total = jnp.zeros((TOK, HD), F32)
@@ -413,17 +428,21 @@
     for copy in t_copies:
         copy.start()
 
+    l_third = sum_planes(gb2, gl3, (l3_s, l3_r))
+    l_second[0].wait_recv()
+    add_second(gb1, gl2, gb2, 0, FAR_COUNT)
+    for copy in l_third[:FAR_COUNT]:
+        copy.start()
+    l_second[1].wait_recv()
+    add_second(gb1, gl2, gb2, FAR_COUNT, PLANES)
+    for copy in l_third[FAR_COUNT:]:
+        copy.start()
+
     for copy in e_third:
         copy.wait_recv()
     early = add_third(ga2, ge3)
     g1[:, 0:HD] = early[:, 0:HD]
     g2[...] = early[:, HD:]
-
-    l_second.wait_recv()
-    add_second(gb1, gl2, gb2)
-    l_third = sum_planes(gb2, gl3, (l3_s, l3_r))
-    for copy in l_third:
-        copy.start()
 
     summed = own[...]
     for i, copy in p_copies:
@@ -446,7 +465,7 @@
         hop_upstream(d, by).wait_send()
     for i, copy in p_copies:
         copy.wait_send()
-    for copy in (e_first, e_second, k_first, k_second, l_first, l_second):
+    for copy in e_second + l_second + [e_first, k_first, k_second, l_first]:
         copy.wait_send()
 
     for copy in l_third:
@@ -511,7 +530,7 @@
         pltpu.VMEM((8, TOK), F32),
         pltpu.VMEM((HEADS, 8, TOK), F32),
     ]
-    counts = (8, 8, 5, 5, 5, 5, 4, 4, 5, 5, 2, 2, 2, 2, 16, 16, 2, 2, 16, 16, 8, 8, 8, 8)
+    counts = (8, 8, 5, 5, 5, 5, 4, 4, 5, 5, 2, 2, 3, 3, 16, 16, 3, 3, 16, 16, 8, 8, 8, 8)
     scratch += [dma((6,)), pltpu.SemaphoreType.REGULAR((3,))]
     scratch += [dma((n,)) for n in counts]
     return pl.pallas_call(

time: 78.7 us -> 76 us (0.966)
  Pallas kernels: 75 us -> 72.3 us
    pallas_call x1, Pallas kernels: 75 us -> 72.3 us  [per_device(): pl.pallas_call(kernel, out_shape=(jax.ShapeDtypeStruct(tile, BF16), jax.S...]
where the time goes in v6:
time: 76 us; the launch traced here: 75.7 us
  Pallas kernels  72.3 us (95%)
  local copies, waits for them, and re-layouts  2.79 us (4%)
    pallas_call x1, Pallas kernels, per_device(): pl.pallas_call(kernel, out_shape=(jax.ShapeDtypeStruct(tile, BF16), jax.S...  72.3 us
    unnamed x7, local copies, waits for them, and re-layouts  2.79 us

profile of v6, /device:TPU:1, one launch (start us, length us, event | category | flops | bytes accessed | tf_op | source)
XLA Modules:
  0.0 75.7 jit_solution(16884324047750882553)
XLA Ops:
  0.6 72.3 %layer_backward.1 = (bf16[256,128]{1,0:T(8,128)(2,1)}, f32[16,512]{1,0:T(8,128)}, f32[16,128]{1,0:T(8,128)}) custom-call(bf16[256,1024]{1,0:T(8,128)(2,1)} %ev_h.1, bf16[256,128]{1,0:T(8,128)(2,1)} %og_h.1, bf16[256,128]{1,0:T(8,128)(2,1)} %sa_h.1, bf16[1024,512]{1,0:T(8,128)(2,1)} %wi_h.1, bf16[1024,128]{1,0:T(8,128)(2,1)} %wo_h.1, s32[16]{0:T(128)} %lens_h.1), custom_call_target="tpu_custom_call" | custom-call | tf_op jit(solution)/shard_map/layer_backward/pallas_call | solution.py:536
  72.9 0.0 copy-start
  72.9 1.5 %copy.12 = bf16[256,128]{1,0:T(8,128)(2,1)} copy(bf16[256,128]{1,0:T(8,128)(2,1)} %get-tuple-element.6) | data formatting | bytes 131072
  74.4 0.0 copy-done
  74.4 0.0 copy-start.1
  74.4 0.6 copy.13
  75.0 0.1 copy-done.1
  75.1 0.6 copy.14
Async XLA Ops:
  72.9 1.5 %copy-start = (f32[16,512]{1,0:T(8,128)S(1)}, f32[16,512]{1,0:T(8,128)}, u32[]{:S(2)}) copy-start(f32[16,512]{1,0:T(8,128)} %get-tuple-element.7) | copy-start | bytes 98308
  74.4 0.7 copy-start.1

commit v7 on v6

--- a/solution.py
+++ b/solution.py
@@ -292,17 +292,16 @@
         return place + row % 256
 
     rowpos[...] = slot_rows((4 * TOK, HD))
-
-    def attend(d, same):
+    kvg[...] = jnp.zeros_like(kvg)
+
+    def attend(d):
         queries = qa[d]
         upstream = doa[d]
         keys = kva[:, 0].reshape(4 * TOK, HD)
         values = kva[:, 1].reshape(4 * TOK, HD)
         down = jnp.concatenate([rowpos[...]] * 2, axis=1)
-        mask = down >= begin[d, 0:1, :]
-        if same:
-            lane = lax.broadcasted_iota(jnp.int32, (1, TOK), 1)
-            mask = mask & (down <= xh * 512 + c * 256 + lane)
+        lane = lax.broadcasted_iota(jnp.int32, (1, TOK), 1)
+        mask = (down >= begin[d, 0:1, :]) & (down <= d * 1024 + xh * 512 + c * 256 + lane)
         half = nt(keys, queries) * (0.5 * SCALE)
         bell = 1.0 + jnp.tanh(half)
         weight = half * bell
@@ -312,28 +311,18 @@
         weight = jnp.where(mask, weight, 0.0).astype(BF16)
         grad_k = nn(dscore, queries).reshape(4, TOK, HD)
         grad_v = nn(weight, upstream).reshape(4, TOK, HD)
-        if same:
-            kvg[:, 0] = grad_k
-            kvg[:, 1] = grad_v
-        else:
-            kvg[:, 0] += grad_k
-            kvg[:, 1] += grad_v
+        kvg[:, 0] += grad_k
+        kvg[:, 1] += grad_v
         dqs[d] = nn(ktr[...], dscore).astype(BF16)
 
     hop_upstream(0, 2).wait_recv()
     hop_upstream(2, 2).start()
     hop_upstream(0, 1).wait_recv()
     hop_upstream(1, 2).start()
-    attend(0, True)
-
-    e_first.wait_recv()
-    add_first(ge, ge1, ga1)
     e_second = sum_across(ga1, ge2, (e12_s, e12_r))
-    for copy in e_second:
-        copy.start()
 
     def attend_step(turn, carry):
-        d = jnp.where(turn < 2, 2 - turn, 6 - turn)
+        d = jnp.where(turn < 3, 2 - turn, 7 - turn)
 
         @pl.when(d == 4)
         def _():
@@ -345,11 +334,22 @@
             hop_queries(1, 2).wait_recv()
             hop_upstream(1, 2).wait_recv()
 
-        attend(d, False)
-        push(dqs.at[d], dqr.at[d], dq_s.at[d], dq_r.at[d], at_z(d)).start()
+        attend(d)
+
+        @pl.when(d > 0)
+        def _():
+            push(dqs.at[d], dqr.at[d], dq_s.at[d], dq_r.at[d], at_z(d)).start()
+
+        @pl.when(d == 0)
+        def _():
+            e_first.wait_recv()
+            add_first(ge, ge1, ga1)
+            for copy in e_second:
+                copy.start()
+
         return carry
 
-    lax.fori_loop(0, REACH, attend_step, 0)
+    lax.fori_loop(0, REACH + 1, attend_step, 0)
 
     for j in range(2):
         other = 2 * j + 1
@@ -371,17 +371,6 @@
     dq_copies = [
         push(dqs.at[d], dqr.at[d], dq_s.at[d], dq_r.at[d], at_z(d)) for d in range(1, REACH + 1)
     ]
-    grad_q = dqs[0].astype(F32)
-    for d in range(REACH, 0, -1):
-        dq_copies[d - 1].wait_recv()
-        grad_q += dqr[d].astype(F32)
-    for copy in e_third:
-        copy.start()
-    dproj[:, 2 * HD : 3 * HD] = (grad_q.T * (SCALE / MOST) * slope[2]).astype(BF16)
-    gl[:, :, :, 2 * HD :] = (
-        nn(ntr[...], dproj[:, 2 * HD : 3 * HD]).astype(BF16).reshape(32, 2, 16, HD)
-    )
-
     k_second.wait_recv()
     grad_k = kvg[0, 0] + kvr1[0, 0].astype(F32) + kvr2[0].astype(F32)
     grad_v = kvg[0, 1] + kvr1[0, 1].astype(F32) + kvr2[1].astype(F32)
@@ -389,8 +378,19 @@
     dproj[:, HD : 2 * HD] = (grad_v * (1.0 / MOST) * slope[1]).astype(BF16)
     pair = jnp.concatenate([dproj[:, HD : 2 * HD], dproj[:, 3 * HD :]], axis=1)
     gl[:, :, :, 0 : 2 * HD] = nn(ntr[...], pair).astype(BF16).reshape(32, 2, 16, 2 * HD)
+    grad_q = dqs[0].astype(F32)
+    for d in range(REACH, 0, -1):
+        dq_copies[d - 1].wait_recv()
+        grad_q += dqr[d].astype(F32)
+    dproj[:, 2 * HD : 3 * HD] = (grad_q.T * (SCALE / MOST) * slope[2]).astype(BF16)
+    gl[:, :, :, 2 * HD :] = (
+        nn(ntr[...], dproj[:, 2 * HD : 3 * HD]).astype(BF16).reshape(32, 2, 16, HD)
+    )
+
     l_first = sum_parts(gl, gl1, (l12_s, l12_r))
     l_first.start()
+    for copy in e_third:
+        copy.start()
     l_first.wait_recv()
     add_first(gl, gl1, gb1)
     l_second = sum_across(gb1, gl2, (l12_s, l12_r))

time: 76 us -> 73.5 us (0.967)
  Pallas kernels: 72.3 us -> 69.6 us
    pallas_call x1, Pallas kernels: 72.3 us -> 69.6 us  [per_device(): pl.pallas_call(kernel, out_shape=(jax.ShapeDtypeStruct(tile, BF16), jax.S...]
where the time goes in v7:
time: 73.5 us; the launch traced here: 73 us
  Pallas kernels  69.6 us (95%)
  local copies, waits for them, and re-layouts  2.79 us (4%)
    pallas_call x1, Pallas kernels, per_device(): pl.pallas_call(kernel, out_shape=(jax.ShapeDtypeStruct(tile, BF16), jax.S...  69.6 us
    unnamed x7, local copies, waits for them, and re-layouts  2.79 us

profile of v7, /device:TPU:1, one launch (start us, length us, event | category | flops | bytes accessed | tf_op | source)
XLA Modules:
  0.0 73.0 jit_solution(9102270916423190840)
XLA Ops:
  0.6 69.6 %layer_backward.1 = (bf16[256,128]{1,0:T(8,128)(2,1)}, f32[16,512]{1,0:T(8,128)}, f32[16,128]{1,0:T(8,128)}) custom-call(bf16[256,1024]{1,0:T(8,128)(2,1)} %ev_h.1, bf16[256,128]{1,0:T(8,128)(2,1)} %og_h.1, bf16[256,128]{1,0:T(8,128)(2,1)} %sa_h.1, bf16[1024,512]{1,0:T(8,128)(2,1)} %wi_h.1, bf16[1024,128]{1,0:T(8,128)(2,1)} %wo_h.1, s32[16]{0:T(128)} %lens_h.1), custom_call_target="tpu_custom_call" | custom-call | tf_op jit(solution)/shard_map/layer_backward/pallas_call | solution.py:536
  70.2 0.0 copy-start
  70.3 1.5 %copy.12 = bf16[256,128]{1,0:T(8,128)(2,1)} copy(bf16[256,128]{1,0:T(8,128)(2,1)} %get-tuple-element.6) | data formatting | bytes 131072
  71.7 0.0 copy-done
  71.7 0.0 copy-start.1
  71.7 0.6 copy.13
  72.4 0.1 copy-done.1
  72.4 0.6 copy.14
Async XLA Ops:
  70.2 1.5 %copy-start = (f32[16,512]{1,0:T(8,128)S(1)}, f32[16,512]{1,0:T(8,128)}, u32[]{:S(2)}) copy-start(f32[16,512]{1,0:T(8,128)} %get-tuple-element.7) | copy-start | bytes 98308
  71.7 0.7 copy-start.1

commit v8 on v7

--- a/solution.py
+++ b/solution.py
@@ -56,11 +56,11 @@
     fg, qa, doa, kva, ktr, begin, rowpos, kvg, dqs, dqr,
     kvs1, kvr1, kvs2, kvr2,
     ge, ge1, ga1, ge2, ga2, ge3,
-    gl, gl1, gb1, gl2, gb2, gl3,
+    gl, gl1, gb1, gl2, gq, gq1, gc1, gq2, gb2, gl3,
     ps, pr, own, st, sr,
     in_s, near,
     fg_s, fg_r, q_s, q_r, do_s, do_r, kv_s, kv_r, dq_s, dq_r, kx_s, kx_r,
-    e12_s, e12_r, e3_s, e3_r, l12_s, l12_r, l3_s, l3_r, p_s, p_r, t_s, t_r,
+    e12_s, e12_r, e3_s, e3_r, l12_s, l12_r, c12_s, c12_r, l3_s, l3_r, p_s, p_r, t_s, t_r,
 ):
     s = lax.axis_index("seq")
     h = lax.axis_index("head")
@@ -235,9 +235,11 @@
             for i, low, count in ((1, 0, FAR_COUNT), (2, FAR_COUNT, PLANES - FAR_COUNT))
         ]
 
-    def add_second(kept, came, final, low, high):
+    def add_second(kept, came, final, low, high, left=0):
         def step(k, carry):
-            final[k] = (kept[k, xh].astype(F32) + came[k].astype(F32)).astype(BF16)
+            final[k, :, left : left + kept.shape[3]] = (
+                kept[k, xh].astype(F32) + came[k].astype(F32)
+            ).astype(BF16)
             return carry
 
         lax.fori_loop(low, high, step, 0)
@@ -377,24 +379,28 @@
     dproj[:, 3 * HD :] = (grad_k * (SCALE / MOST) * slope[3]).astype(BF16)
     dproj[:, HD : 2 * HD] = (grad_v * (1.0 / MOST) * slope[1]).astype(BF16)
     pair = jnp.concatenate([dproj[:, HD : 2 * HD], dproj[:, 3 * HD :]], axis=1)
-    gl[:, :, :, 0 : 2 * HD] = nn(ntr[...], pair).astype(BF16).reshape(32, 2, 16, 2 * HD)
+    gl[...] = nn(ntr[...], pair).astype(BF16).reshape(32, 2, 16, 2 * HD)
+    l_first = sum_parts(gl, gl1, (l12_s, l12_r))
+    l_first.start()
+    l_first.wait_recv()
+    add_first(gl, gl1, gb1)
+    l_second = sum_across(gb1, gl2, (l12_s, l12_r))
+    for copy in l_second:
+        copy.start()
     grad_q = dqs[0].astype(F32)
     for d in range(REACH, 0, -1):
         dq_copies[d - 1].wait_recv()
         grad_q += dqr[d].astype(F32)
     dproj[:, 2 * HD : 3 * HD] = (grad_q.T * (SCALE / MOST) * slope[2]).astype(BF16)
-    gl[:, :, :, 2 * HD :] = (
-        nn(ntr[...], dproj[:, 2 * HD : 3 * HD]).astype(BF16).reshape(32, 2, 16, HD)
-    )
-
-    l_first = sum_parts(gl, gl1, (l12_s, l12_r))
-    l_first.start()
+    gq[...] = nn(ntr[...], dproj[:, 2 * HD : 3 * HD]).astype(BF16).reshape(32, 2, 16, HD)
+    q_first = sum_parts(gq, gq1, (c12_s, c12_r))
+    q_first.start()
     for copy in e_third:
         copy.start()
-    l_first.wait_recv()
-    add_first(gl, gl1, gb1)
-    l_second = sum_across(gb1, gl2, (l12_s, l12_r))
-    for copy in l_second:
+    q_first.wait_recv()
+    add_first(gq, gq1, gc1)
+    q_second = sum_across(gc1, gq2, (c12_s, c12_r))
+    for copy in q_second:
         copy.start()
 
     total = jnp.zeros((TOK, HD), F32)
@@ -429,12 +435,15 @@
         copy.start()
 
     l_third = sum_planes(gb2, gl3, (l3_s, l3_r))
-    l_second[0].wait_recv()
-    add_second(gb1, gl2, gb2, 0, FAR_COUNT)
+    for copy in l_second:
+        copy.wait_recv()
+    add_second(gb1, gl2, gb2, 0, PLANES)
+    q_second[0].wait_recv()
+    add_second(gc1, gq2, gb2, 0, FAR_COUNT, 2 * HD)
     for copy in l_third[:FAR_COUNT]:
         copy.start()
-    l_second[1].wait_recv()
-    add_second(gb1, gl2, gb2, FAR_COUNT, PLANES)
+    q_second[1].wait_recv()
+    add_second(gc1, gq2, gb2, FAR_COUNT, PLANES, 2 * HD)
     for copy in l_third[FAR_COUNT:]:
         copy.start()
 
@@ -465,7 +474,7 @@
         hop_upstream(d, by).wait_send()
     for i, copy in p_copies:
         copy.wait_send()
-    for copy in e_second + l_second + [e_first, k_first, k_second, l_first]:
+    for copy in e_second + l_second + q_second + [e_first, k_first, k_second, l_first, q_first]:
         copy.wait_send()
 
     for copy in l_third:
@@ -523,14 +532,16 @@
         pltpu.VMEM((2,) + tile, BF16),
         pltpu.VMEM((2,) + tile, BF16),
         *rows_of(2 * HD),
-        *rows_of(3 * HD),
+        *rows_of(2 * HD)[:4],
+        *rows_of(HD)[:4],
+        *rows_of(3 * HD)[4:],
         pltpu.VMEM((HEADS,) + tile, BF16),
         pltpu.VMEM((HEADS,) + tile, BF16),
         pltpu.VMEM(tile, F32),
         pltpu.VMEM((8, TOK), F32),
         pltpu.VMEM((HEADS, 8, TOK), F32),
     ]
-    counts = (8, 8, 5, 5, 5, 5, 4, 4, 5, 5, 2, 2, 3, 3, 16, 16, 3, 3, 16, 16, 8, 8, 8, 8)
+    counts = (8, 8, 5, 5, 5, 5, 4, 4, 5, 5, 2, 2, 3, 3, 16, 16, 3, 3, 3, 3, 16, 16, 8, 8, 8, 8)
     scratch += [dma((6,)), pltpu.SemaphoreType.REGULAR((3,))]
     scratch += [dma((n,)) for n in counts]
     return pl.pallas_call(

time: 73.5 us -> 72.5 us (0.986)
  Pallas kernels: 69.6 us -> 68.8 us
    pallas_call x1, Pallas kernels: 69.6 us -> 68.8 us  [per_device(): pl.pallas_call(kernel, out_shape=(jax.ShapeDtypeStruct(tile, BF16), jax.S...]
where the time goes in v8:
time: 72.5 us; the launch traced here: 72.3 us
  Pallas kernels  68.8 us (95%)
  local copies, waits for them, and re-layouts  2.79 us (4%)
    pallas_call x1, Pallas kernels, per_device(): pl.pallas_call(kernel, out_shape=(jax.ShapeDtypeStruct(tile, BF16), jax.S...  68.8 us
    unnamed x7, local copies, waits for them, and re-layouts  2.79 us

profile of v8, /device:TPU:1, one launch (start us, length us, event | category | flops | bytes accessed | tf_op | source)
XLA Modules:
  0.0 72.3 jit_solution(8973607415226528421)
XLA Ops:
  0.6 68.8 %layer_backward.1 = (bf16[256,128]{1,0:T(8,128)(2,1)}, f32[16,512]{1,0:T(8,128)}, f32[16,128]{1,0:T(8,128)}) custom-call(bf16[256,1024]{1,0:T(8,128)(2,1)} %ev_h.1, bf16[256,128]{1,0:T(8,128)(2,1)} %og_h.1, bf16[256,128]{1,0:T(8,128)(2,1)} %sa_h.1, bf16[1024,512]{1,0:T(8,128)(2,1)} %wi_h.1, bf16[1024,128]{1,0:T(8,128)(2,1)} %wo_h.1, s32[16]{0:T(128)} %lens_h.1), custom_call_target="tpu_custom_call" | custom-call | tf_op jit(solution)/shard_map/layer_backward/pallas_call | solution.py:547
  69.5 0.0 copy-start
  69.5 1.5 %copy.12 = bf16[256,128]{1,0:T(8,128)(2,1)} copy(bf16[256,128]{1,0:T(8,128)(2,1)} %get-tuple-element.6) | data formatting | bytes 131072
  71.0 0.0 copy-done
  71.0 0.0 copy-start.1
  71.0 0.6 copy.13
  71.6 0.1 copy-done.1
  71.7 0.6 copy.14
Async XLA Ops:
  69.5 1.5 %copy-start = (f32[16,512]{1,0:T(8,128)S(1)}, f32[16,512]{1,0:T(8,128)}, u32[]{:S(2)}) copy-start(f32[16,512]{1,0:T(8,128)} %get-tuple-element.7) | copy-start | bytes 98308
  71.0 0.7 copy-start.1
